TPU v7x, 128 devices: a whole 4x4x4 slice. The times are simulated.
128 devices in a mesh: dp: 16 (over z, x_hi, core), tensor: 8 (over x_lo, y).
Axes of the slice: x: 4 (x_hi: 2, x_lo: 2; x = x_hi * 2 + x_lo), y: 4, z: 4, core: 2. Of those that a mesh axis runs over, the one named last changes fastest.
Arguments:
- tokens: bfloat16 [16384, 1024], P(('dp', 'tensor')), may hold values from -6 to 6
- attn_in: bfloat16 [1024, 3, 16, 64], P(None, None, 'tensor'), may hold values from -0.25 to 0.25
- attn_out: bfloat16 [16, 64, 1024], P('tensor'), may hold values from -1 to 1
- mlp_in: bfloat16 [2, 1024, 2624], P(None, None, 'tensor'), may hold values from -0.1875 to 0.1875
- mlp_out: bfloat16 [2624, 1024], P('tensor'), may hold values from -0.25 to 0.25
- norm_first: float32 [1024], replicated, may hold values from 0.5 to 1.5
- norm_second: float32 [1024], replicated, may hold values from 0.5 to 1.5
- cotangent: bfloat16 [16384, 1024], P(('dp', 'tensor')), may hold values from -6 to 6
Outputs:
- layer_output: bfloat16 [16384, 1024], P(('dp', 'tensor'))
- tokens_grad: float32 [16384, 1024], P(('dp', 'tensor'))
- attn_in_grad: float32 [1024, 3, 16, 64], P(None, None, 'tensor')
- attn_out_grad: float32 [16, 64, 1024], P('tensor')
- mlp_in_grad: float32 [2, 1024, 2624], P(None, None, 'tensor')
- mlp_out_grad: float32 [2624, 1024], P('tensor')
- norm_first_grad: float32 [1024], replicated
- norm_second_grad: float32 [1024], replicated
All inputs are finite; a program needn't handle non-finite values.
Results may differ from a plain program's by a relative error of at most 0.03.
Values may be sent and summed in bfloat16 or wider, within the bound.
A program may use at most 128 MiB of HBM per device.

v0:
```python
import jax
import jax.numpy as jnp
from jax import lax
from jax.sharding import PartitionSpec as P

SEQ_LEN = 1024


EPS = 1e-05
THETA = 160000.0


def rope_tables(length, head_size):
    places = jnp.arange(length, dtype=jnp.float32)
    frequency = THETA ** (-jnp.arange(0, head_size, 2, dtype=jnp.float32) / head_size)
    angles = places[:, None] * frequency[None, :]
    cosine = jnp.concatenate([jnp.cos(angles), jnp.cos(angles)], -1)
    sine_table = jnp.concatenate([jnp.sin(angles), jnp.sin(angles)], -1)
    return (cosine[:, None, :], sine_table[:, None, :])


def rotate(values, cosine, sine_table):
    half_size = values.shape[-1] // 2
    turned = jnp.concatenate([-values[..., half_size:], values[..., :half_size]], -1)
    return values * cosine + turned * sine_table


def rotate_back(gradient, cosine, sine_table):
    half_size = gradient.shape[-1] // 2
    scaled = gradient * sine_table
    turned = jnp.concatenate([scaled[..., half_size:], -scaled[..., :half_size]], -1)
    return gradient * cosine + turned


def norm_forward(values, gain_vector):
    row_mean = jnp.mean(values, -1, keepdims=True)
    centred = values - row_mean
    inverse = lax.rsqrt(jnp.mean(centred * centred, -1, keepdims=True) + EPS)
    normed = centred * inverse
    return ((normed * gain_vector).astype(jnp.bfloat16), normed, inverse)


def norm_backward(gradient, normed, inverse, gain_vector):
    grad_hat = gradient * gain_vector
    inner = (
        grad_hat
        - jnp.mean(grad_hat, -1, keepdims=True)
        - normed * jnp.mean(grad_hat * normed, -1, keepdims=True)
    )
    return (inverse * inner, jnp.sum(gradient * normed, 0))


def geglu(gate_part, up_part):
    return jax.nn.gelu(gate_part, approximate=False) * up_part


def local(tokens, attn_in, attn_out, mlp_in, mlp_out, norm_first, norm_second, cotangent):
    local_rows, model_width = tokens.shape
    total_rows = local_rows * lax.axis_size("tensor")
    seq_count = total_rows // SEQ_LEN
    head_count = attn_in.shape[2]
    head_size = attn_in.shape[3]
    inner_width = head_count * head_size
    score_scale = head_size ** (-0.5)
    block_rows = min(512, SEQ_LEN)
    block_count = SEQ_LEN // block_rows
    cosine, sine_table = rope_tables(SEQ_LEN, head_size)
    seq_shape = (seq_count, SEQ_LEN, head_count, head_size)
    block_shape = (block_count, block_rows, head_count, head_size)
    inflow = tokens.astype(jnp.float32)
    first_hidden, first_normed, first_inverse = norm_forward(inflow, norm_first)
    first_all = lax.all_gather(first_hidden, "tensor", axis=0, tiled=True)
    proj_weight = attn_in.reshape(model_width, 3 * inner_width)
    projected = jnp.dot(first_all, proj_weight, preferred_element_type=jnp.float32)
    projected = projected.reshape(seq_count, SEQ_LEN, 3, head_count, head_size)
    queries = rotate(projected[:, :, 0], cosine, sine_table).astype(jnp.bfloat16)
    key_rows = rotate(projected[:, :, 1], cosine, sine_table).astype(jnp.bfloat16)
    value_rows = projected[:, :, 2].astype(jnp.bfloat16)

    def sequence_forward(operands):
        seq_queries, seq_keys, seq_values = operands

        def block_forward(query_block):
            scores = (
                jnp.einsum(
                    "qhe,khe->hqk", query_block, seq_keys, preferred_element_type=jnp.float32
                )
                * score_scale
            )
            top_score = jnp.max(scores, -1, keepdims=True)
            powers = jnp.exp(scores - top_score)
            row_total = jnp.sum(powers, -1, keepdims=True)
            probs = (powers / row_total).astype(jnp.bfloat16)
            outcome = jnp.einsum(
                "hqk,khe->qhe", probs, seq_values, preferred_element_type=jnp.float32
            )
            return (outcome, (top_score + jnp.log(row_total))[..., 0])

        outcome, log_sums = lax.map(block_forward, seq_queries.reshape(block_shape))
        return (outcome.reshape(SEQ_LEN, head_count, head_size), log_sums)

    attended, log_sums = lax.map(sequence_forward, (queries, key_rows, value_rows))
    attended = attended.reshape(total_rows, inner_width).astype(jnp.bfloat16)
    out_weight = attn_out.reshape(inner_width, model_width)
    piece = attended
    middle = inflow + lax.psum_scatter(
        jnp.dot(piece, out_weight, preferred_element_type=jnp.float32).astype(jnp.bfloat16),
        "tensor",
        scatter_dimension=0,
        tiled=True,
    ).astype(jnp.float32)
    second_hidden, second_normed, second_inverse = norm_forward(middle, norm_second)
    second_all = lax.all_gather(second_hidden, "tensor", axis=0, tiled=True)
    gate_part = jnp.dot(second_all, mlp_in[0], preferred_element_type=jnp.float32)
    up_part = jnp.dot(second_all, mlp_in[1], preferred_element_type=jnp.float32)
    mixed, geglu_pull = jax.vjp(geglu, gate_part, up_part)
    mixed = mixed.astype(jnp.bfloat16)
    piece = mixed
    layer_output = (
        middle
        + lax.psum_scatter(
            jnp.dot(piece, mlp_out, preferred_element_type=jnp.float32).astype(jnp.bfloat16),
            "tensor",
            scatter_dimension=0,
            tiled=True,
        ).astype(jnp.float32)
    ).astype(jnp.bfloat16)
    upstream = cotangent.astype(jnp.float32)
    upstream_all = lax.all_gather(cotangent, "tensor", axis=0, tiled=True)
    mlp_out_grad = jnp.einsum("tf,td->fd", mixed, upstream_all, preferred_element_type=jnp.float32)
    mixed_grad = jnp.einsum("td,fd->tf", upstream_all, mlp_out, preferred_element_type=jnp.float32)
    mixed_grad = mixed_grad.astype(jnp.bfloat16).astype(jnp.float32)
    gate_grad, up_grad = geglu_pull(mixed_grad)
    gate_grad = gate_grad.astype(jnp.bfloat16)
    up_grad = up_grad.astype(jnp.bfloat16)
    mlp_in_grad = jnp.stack(
        [
            jnp.einsum("td,tf->df", second_all, gate_grad, preferred_element_type=jnp.float32),
            jnp.einsum("td,tf->df", second_all, up_grad, preferred_element_type=jnp.float32),
        ]
    )
    second_grad = lax.psum_scatter(
        (
            jnp.einsum("tf,df->td", gate_grad, mlp_in[0], preferred_element_type=jnp.float32)
            + jnp.einsum("tf,df->td", up_grad, mlp_in[1], preferred_element_type=jnp.float32)
        ).astype(jnp.bfloat16),
        "tensor",
        scatter_dimension=0,
        tiled=True,
    ).astype(jnp.float32)
    middle_part, second_gain = norm_backward(
        second_grad, second_normed, second_inverse, norm_second
    )
    middle_grad = upstream + middle_part
    middle_all = lax.all_gather(middle_grad.astype(jnp.bfloat16), "tensor", axis=0, tiled=True)
    attn_out_grad = jnp.einsum(
        "tc,td->cd", attended, middle_all, preferred_element_type=jnp.float32
    )
    attn_out_grad = attn_out_grad.reshape(head_count, head_size, model_width)
    attended_grad = jnp.einsum(
        "td,cd->tc", middle_all, out_weight, preferred_element_type=jnp.float32
    )
    attended_grad = attended_grad.astype(jnp.bfloat16).reshape(seq_shape)

    def sequence_backward(operands):
        seq_queries, seq_keys, seq_values, seq_grad, seq_logs = operands

        def block_backward(carry, pieces):
            key_total, value_total = carry
            query_block, grad_block, log_block = pieces
            scores = (
                jnp.einsum(
                    "qhe,khe->hqk", query_block, seq_keys, preferred_element_type=jnp.float32
                )
                * score_scale
            )
            probs = jnp.exp(scores - log_block[..., None])
            low_probs = probs.astype(jnp.bfloat16)
            prob_grad = jnp.einsum(
                "qhe,khe->hqk", grad_block, seq_values, preferred_element_type=jnp.float32
            )
            weighted = jnp.sum(probs * prob_grad, -1, keepdims=True)
            score_grad = (probs * (prob_grad - weighted)).astype(jnp.bfloat16)
            query_grad = (
                jnp.einsum("hqk,khe->qhe", score_grad, seq_keys, preferred_element_type=jnp.float32)
                * score_scale
            )
            key_total = (
                key_total
                + jnp.einsum(
                    "hqk,qhe->khe", score_grad, query_block, preferred_element_type=jnp.float32
                )
                * score_scale
            )
            value_total = value_total + jnp.einsum(
                "hqk,qhe->khe", low_probs, grad_block, preferred_element_type=jnp.float32
            )
            return ((key_total, value_total), query_grad)

        start_carry = (
            jnp.zeros((SEQ_LEN, head_count, head_size), jnp.float32),
            jnp.zeros((SEQ_LEN, head_count, head_size), jnp.float32),
        )
        (key_grad, value_grad), query_grads = lax.scan(
            block_backward,
            start_carry,
            (seq_queries.reshape(block_shape), seq_grad.reshape(block_shape), seq_logs),
        )
        return (query_grads.reshape(SEQ_LEN, head_count, head_size), key_grad, value_grad)

    query_grad, key_grad, value_grad = lax.map(
        sequence_backward, (queries, key_rows, value_rows, attended_grad, log_sums)
    )
    projected_grad = jnp.stack(
        [
            rotate_back(query_grad, cosine, sine_table),
            rotate_back(key_grad, cosine, sine_table),
            value_grad,
        ],
        2,
    )
    projected_grad = projected_grad.astype(jnp.bfloat16).reshape(total_rows, 3 * inner_width)
    attn_in_grad = jnp.einsum(
        "td,tc->dc", first_all, projected_grad, preferred_element_type=jnp.float32
    )
    attn_in_grad = attn_in_grad.reshape(model_width, 3, head_count, head_size)
    piece = projected_grad
    first_grad = lax.psum_scatter(
        jnp.einsum("tc,dc->td", piece, proj_weight, preferred_element_type=jnp.float32).astype(
            jnp.bfloat16
        ),
        "tensor",
        scatter_dimension=0,
        tiled=True,
    ).astype(jnp.float32)
    inflow_part, first_gain = norm_backward(first_grad, first_normed, first_inverse, norm_first)
    tokens_grad = middle_grad + inflow_part
    attn_in_grad, attn_out_grad, mlp_in_grad, mlp_out_grad = (
        lax.psum(attn_in_grad.astype(jnp.bfloat16), "dp").astype(jnp.float32),
        lax.psum(attn_out_grad.astype(jnp.bfloat16), "dp").astype(jnp.float32),
        lax.psum(mlp_in_grad.astype(jnp.bfloat16), "dp").astype(jnp.float32),
        lax.psum(mlp_out_grad.astype(jnp.bfloat16), "dp").astype(jnp.float32),
    )
    first_gain, second_gain = lax.psum((first_gain, second_gain), ("dp", "tensor"))
    return (
        layer_output,
        tokens_grad,
        attn_in_grad,
        attn_out_grad,
        mlp_in_grad,
        mlp_out_grad,
        first_gain,
        second_gain,
    )


def solution(mesh):
    placed = (
        P(("dp", "tensor"), None),
        P(None, None, "tensor", None),
        P("tensor", None, None),
        P(None, None, "tensor"),
        P("tensor", None),
        P(),
        P(),
        P(("dp", "tensor"), None),
    )
    return jax.shard_map(
        local,
        mesh=mesh,
        in_specs=placed,
        out_specs=(
            P(("dp", "tensor"), None),
            P(("dp", "tensor"), None),
            P(None, None, "tensor", None),
            P("tensor", None, None),
            P(None, None, "tensor"),
            P("tensor", None),
            P(),
            P(),
        ),
        check_vma=False,
    )
```

profile of v0, /device:TPU:1, one launch (start us, length us, event | category | flops | bytes accessed | tf_op | source)
XLA Modules:
  0.0 618.7 jit_solution(9734710550416389121)
XLA Ops:
  7.2 1.1 convert_reduce_fusion
  8.4 1.2 fusion.91
  9.6 1.9 fusion.87
  13.6 37.5 %all-gather.5.cloned.1.call-done = bf16[1024,1024]{1,0:T(8,128)(2,1)} async-done(((bf16[128,1024]{1,0:T(8,128)(2,1)}), bf16[1024,1024]{1,0:T(8,128)(2,1)}) %all-gather.5.cloned.1.call-update) | async-done | bytes 2097168 | tf_op jit(solution)/shard_map/all_gather | solution.py:72
  51.1 2.6 fusion.44
  53.7 1.2 slice_bitcast_fusion
  55.7 2.3 squeeze.50
  58.0 1.9 slice_negate_fusion.3
  59.9 1.2 concatenate.84
  61.8 1.2 concatenate.85
  63.1 1.2 fusion.102
  65.3 5.9 while.47
  66.1 0.9 fusion.166
  67.1 1.1 fusion.167
  70.0 1.1 fusion.167
  72.3 2.1 convolution_convert_fusion.2
  74.4 42.0 %reduce-scatter.5.cloned.1.call-done = bf16[128,1024]{1,0:T(8,128)(2,1)} async-done(((bf16[1024,1024]{1,0:T(8,128)(2,1)}), bf16[128,1024]{1,0:T(8,128)(2,1)}) %reduce-scatter.5.cloned.1.call-update) | async-done | bytes 262160 | tf_op jit(solution)/shard_map/reduce_scatter | solution.py:106
  116.4 1.1 fusion.106
  117.5 1.2 multiply_reduce_fusion.2
  119.2 1.8 multiply_convert_fusion.2
  121.9 39.6 %all-gather.7.cloned.1.call-done = bf16[1024,1024]{1,0:T(8,128)(2,1)} async-done(((bf16[128,1024]{1,0:T(8,128)(2,1)}), bf16[1024,1024]{1,0:T(8,128)(2,1)}) %all-gather.7.cloned.1.call-update) | async-done | bytes 2097168 | tf_op jit(solution)/shard_map/all_gather | solution.py:113
  161.4 3.6 fusion.71
  165.0 38.7 %all-gather.9.cloned.1.call-done = bf16[1024,1024]{1,0:T(8,128)(2,1)} async-done(((bf16[128,1024]{1,0:T(8,128)(2,1)}), bf16[1024,1024]{1,0:T(8,128)(2,1)}) %all-gather.9.cloned.1.call-update) | async-done | bytes 2097168 | tf_op jit(solution)/shard_map/all_gather | solution.py:129
  203.7 5.8 fusion.50
  209.6 2.3 add_convert_fusion.1
  212.0 1.3 fusion.69
  213.3 2.7 add_convert_fusion
  216.1 42.1 %reduce-scatter.9.cloned.1.call-done = bf16[128,1024]{1,0:T(8,128)(2,1)} async-done(((bf16[1024,1024]{1,0:T(8,128)(2,1)}), bf16[128,1024]{1,0:T(8,128)(2,1)}) %reduce-scatter.9.cloned.1.call-update) | async-done | bytes 262160 | tf_op jit(solution)/shard_map/reduce_scatter | solution.py:142
  258.2 1.9 fusion.96
  260.1 1.9 fusion.117
  262.4 2.6 fusion.57
  265.9 1.2 pad_maximum_fusion
  267.1 0.9 copy-done.55
  268.1 1.7 convolution_convert_fusion.3
  269.8 32.6 %all-gather.11.cloned.1.call-done = bf16[1024,1024]{1,0:T(8,128)(2,1)} async-done(((bf16[128,1024]{1,0:T(8,128)(2,1)}), bf16[1024,1024]{1,0:T(8,128)(2,1)}) %all-gather.11.cloned.1.call-update) | async-done | bytes 2097168 | tf_op jit(solution)/shard_map/all_gather | solution.py:155
  302.4 2.3 convolution_convert_fusion.7
  304.7 1.1 reshape.409
  305.8 1.3 copy.28
  307.0 23.4 %while.48 = (s32[]{:T(128)}, f32[1024,2,64]{0,2,1:T(8,128)S(1)}, f32[1024,2,64]{0,2,1:T(8,128)S(1)}, f32[2,512,2,64]{1,0,3,2:T(2,128)}, bf16[2,512,2,64]{1,3,2,0...) while((s32[]{:T(128)}, f32[1024,2,64]{0,2,1:T(8,128)S(1)}, ...), condition=%wide.region_15.16_spmd.clone, body=%wide.region_13.15_spmd.clone.sunk | while | flops 684391424 | bytes 36204692 | solution.py:204
  307.8 1.0 fusion.179
  308.8 1.4 multiply_reduce_fusion.6
  310.3 1.1 multiply_convert_fusion.4
  313.0 5.8 dynamic_update_slice.31
  319.5 1.0 fusion.179
  320.5 1.4 multiply_reduce_fusion.6
  322.0 1.1 multiply_convert_fusion.4
  324.7 5.8 dynamic_update_slice.31
  330.4 2.4 broadcast_in_dim.48
  332.8 1.2 broadcast_in_dim.47
  336.4 1.3 copy-done.4
  337.7 1.1 fusion.59
  338.9 1.9 fusion.47
  341.9 2.6 convolution_convert_fusion
  344.6 1.0 copy-done.56
  345.8 2.6 convolution_convert_fusion.1
  348.5 147.2 %all-reduce.4.cloned.1.call-done = (bf16[1024,3,2,64]{0,3,2,1:T(8,128)(2,1)}, bf16[2,64,1024]{2,1,0:T(8,128)(2,1)}, bf16[2,1024,328]{1,2,0:T(8,128)(2,1)}, bf16[328,1024]{1,0:T(8,128)(2,1)}) async-done(((bf16[1024,3,2,64]{0,3,2,1:T(8,128)(2,1)}, bf16[2,64,1024]{2,1,0:T(8,128)(2,1)}, bf16[2,1024,328]{1,2,0:T(8,128)(2,1)}, bf16[328,1024]{1,0:T(8,128)(2,1)}), (bf16[1024,3,2,64]{0,3,2,1:T(8,128)(2,1)}, ...) | async-done | bytes 3063824 | tf_op jit(solution)/shard_map/psum | solution.py:239
  495.7 1.8 convert_element_type.169
  497.5 2.5 convert_element_type.167
  500.0 1.2 convert_element_type.172
  501.9 1.8 convert_element_type.170
  503.8 33.3 %reduce-scatter.11.cloned.1.call-done = bf16[128,1024]{1,0:T(8,128)(2,1)} async-done(((bf16[1024,1024]{1,0:T(8,128)(2,1)}), bf16[128,1024]{1,0:T(8,128)(2,1)}) %reduce-scatter.11.cloned.1.call-update) | async-done | bytes 262160 | tf_op jit(solution)/shard_map/reduce_scatter | solution.py:228
  537.1 1.2 fusion.98
  538.3 71.4 %all-reduce = (f32[1024]{0:T(1024)}, f32[1024]{0:T(1024)}) all-reduce(f32[1024]{0:T(1024)S(1)} %get-tuple-element.190, f32[1024]{0:T(1024)S(1)} %copy-done.37), channel_id=1, replica_groups=mesh['dp'=16,'tensor'=8] {'dp','tensor'}, use_global_device_ids=true, to_apply=%region_24.25 | all-reduce | flops 2048 | bytes 16384 | tf_op jit(solution)/shard_map/psum | solution.py:244
  609.9 2.3 fusion.90
  (188 shorter events, 20.2 us)
Async XLA Ops:
  7.2 43.9 %copy-start = (bf16[1024,3,2,64]{0,3,2,1:T(8,128)(2,1)S(1)}, bf16[1024,3,2,64]{0,3,2,1:T(8,128)(2,1)}, u32[]{:S(2)}) copy-start(bf16[1024,3,2,64]{0,3,2,1:T(8,128)(2,1)} %param.13) | copy-start | bytes 2359300
  7.2 43.9 %all-gather.5.cloned.1.call-start = ((), (), s32[]{:S(2)}) async-start(), calls=%async_computation.4 | async-start | bytes 2359296 | tf_op jit(solution)/shard_map/all_gather | solution.py:72
  8.4 3.7 copy-start.44
  9.6 2.6 copy-start.46
  11.5 104.9 %reduce-scatter.5.cloned.1.call-start = ((), (), s32[]{:S(2)}) async-start(), calls=%async_computation.5 | async-start | bytes 2359296 | tf_op jit(solution)/shard_map/reduce_scatter | solution.py:106
  12.2 50.9 %copy-start.5 = (f32[1024,64]{0,1:T(8,128)}, f32[1024,64]{0,1:T(8,128)S(1)}, u32[]{:S(2)}) copy-start(f32[1024,64]{0,1:T(8,128)S(1)} %get-tuple-element.260) | copy-start | bytes 786436
  12.2 50.9 %copy-start.8 = (f32[1024,64]{0,1:T(8,128)}, f32[1024,64]{0,1:T(8,128)S(1)}, u32[]{:S(2)}) copy-start(f32[1024,64]{0,1:T(8,128)S(1)} %get-tuple-element.261) | copy-start | bytes 786436
  63.0 1.4 copy-start.15
  63.0 1.4 copy-start.23
  63.0 1.4 copy-start.24
  63.0 1.4 copy-start.25
  65.3 7.0 %copy-start.21 = (bf16[2,64,1024]{2,1,0:T(8,128)(2,1)S(1)}, bf16[2,64,1024]{2,1,0:T(8,128)(2,1)}, u32[]{:S(2)}) copy-start(bf16[2,64,1024]{2,1,0:T(8,128)(2,1)} %param.14) | copy-start | bytes 786436
  71.2 3.1 copy-start.34
  74.3 42.1 %copy-start.1 = (bf16[128,1024]{1,0:T(8,128)(2,1)S(1)}, bf16[128,1024]{1,0:T(8,128)(2,1)}, u32[]{:S(2)}) copy-start(bf16[128,1024]{1,0:T(8,128)(2,1)} %param.12) | copy-start | bytes 786436
  74.3 44.9 %copy-start.31 = (f32[1024]{0:T(1024)S(1)}, f32[1024]{0:T(1024)}, u32[]{:S(2)}) copy-start(f32[1024]{0:T(1024)} %param.18) | copy-start | bytes 12292
  74.3 87.1 %copy-start.18 = (bf16[2,1024,328]{1,2,0:T(8,128)(2,1)S(1)}, bf16[2,1024,328]{1,2,0:T(8,128)(2,1)}, u32[]{:S(2)}) copy-start(bf16[2,1024,328]{1,2,0:T(8,128)(2,1)} %param.15) | copy-start | bytes 4030468
  74.4 87.1 %all-gather.7.cloned.1.call-start = ((), (), s32[]{:S(2)}) async-start(), calls=%async_computation.6 | async-start | bytes 2359296 | tf_op jit(solution)/shard_map/all_gather | solution.py:113
  117.5 1.2 copy-start.38
  121.1 82.7 %all-gather.9.cloned.1.call-start = ((), (), s32[]{:S(2)}) async-start(), calls=%async_computation.8 | async-start | bytes 2359296 | tf_op jit(solution)/shard_map/all_gather | solution.py:129
  121.6 136.6 %reduce-scatter.9.cloned.1.call-start = ((), (), s32[]{:S(2)}) async-start(), calls=%async_computation.9 | async-start | bytes 2359296 | tf_op jit(solution)/shard_map/reduce_scatter | solution.py:142
  203.7 5.9 copy-start.19
  203.7 5.9 copy-start.53
  203.7 5.9 copy-start.59
  209.6 3.7 copy-start.28
  216.0 42.2 %copy-start.2 = (bf16[128,1024]{1,0:T(8,128)(2,1)S(1)}, bf16[128,1024]{1,0:T(8,128)(2,1)}, u32[]{:S(2)}) copy-start(bf16[128,1024]{1,0:T(8,128)(2,1)} %reduce-scatter.5.cloned.1.call-done) | copy-start | bytes 786436
  216.0 42.2 %copy-start.32 = (f32[1024]{0:T(1024)S(1)}, f32[1024]{0:T(1024)}, u32[]{:S(2)}) copy-start(f32[1024]{0:T(1024)} %param.18) | copy-start | bytes 12292
  216.0 42.2 %copy-start.39 = (f32[128]{0:T(128)S(1)}, f32[128]{0:T(128)}, u32[]{:S(2)}) copy-start(f32[128]{0:T(128)} %copy-done.38) | copy-start | bytes 1540
  216.0 42.2 %copy-start.42 = (f32[128]{0:T(128)S(1)}, f32[128]{0:T(128)}, u32[]{:S(2)}) copy-start(f32[128]{0:T(128)} %copy-done.41) | copy-start | bytes 1540
  216.0 44.1 %copy-start.11 = (bf16[128,1024]{1,0:T(8,128)(2,1)S(1)}, bf16[128,1024]{1,0:T(8,128)(2,1)}, u32[]{:S(2)}) copy-start(bf16[128,1024]{1,0:T(8,128)(2,1)} %param.19) | copy-start | bytes 786436
  216.0 86.4 %all-gather.11.cloned.1.call-start = ((), (), s32[]{:S(2)}) async-start(), calls=%async_computation.10 | async-start | bytes 2359296 | tf_op jit(solution)/shard_map/all_gather | solution.py:155
  260.1 2.3 copy-start.48
  260.1 2.3 copy-start.50
  262.1 233.6 %all-reduce.4.cloned.1.call-start = ((), (), s32[]{:S(2)}) async-start(), calls=%async_computation.12 | async-start | bytes 6127616 | tf_op jit(solution)/shard_map/psum | solution.py:239
  262.4 2.6 copy-start.29
  262.4 2.6 copy-start.54
  265.0 2.1 copy-start.57
  265.9 2.1 copy-start.55
  268.1 34.3 %copy-start.22 = (bf16[2,64,1024]{2,1,0:T(8,128)(2,1)S(1)}, bf16[2,64,1024]{2,1,0:T(8,128)(2,1)}, u32[]{:S(2)}) copy-start(bf16[2,64,1024]{2,1,0:T(8,128)(2,1)} %param.14) | copy-start | bytes 786436
  304.7 2.3 copy-start.35
  330.4 2.4 copy-start.7
  330.4 3.7 copy-start.9
  334.1 1.0 copy-start.17
  335.2 1.1 copy-start.16
  336.1 1.6 copy-start.4
  336.1 1.6 copy-start.14
  336.4 2.4 copy-start.52
  340.8 196.3 %reduce-scatter.11.cloned.1.call-start = ((), (), s32[]{:S(2)}) async-start(), calls=%async_computation.11 | async-start | bytes 2359296 | tf_op jit(solution)/shard_map/reduce_scatter | solution.py:228
  344.5 1.1 copy-start.56
  344.5 1.3 copy-start.58
  344.6 265.2 %reduce-scatter.7.cloned.1.call-start = ((), (), s32[]{:S(2)}) async-start(), calls=%async_computation.7 | async-start | bytes 2359296 | tf_op jit(solution)/shard_map/reduce_scatter | solution.py:121
  497.5 2.5 copy-start.27
  500.0 1.8 copy-start.20
  501.8 35.2 %copy-start.36 = (f32[1024]{0:T(1024)S(1)}, f32[1024]{0:T(1024)}, u32[]{:S(2)}) copy-start(f32[1024]{0:T(1024)} %param.17) | copy-start | bytes 12292
  501.8 35.2 %copy-start.45 = (f32[128]{0:T(128)S(1)}, f32[128]{0:T(128)}, u32[]{:S(2)}) copy-start(f32[128]{0:T(128)} %copy-done.44) | copy-start | bytes 1540
  501.8 35.3 %copy-start.47 = (f32[128]{0:T(128)S(1)}, f32[128]{0:T(128)}, u32[]{:S(2)}) copy-start(f32[128]{0:T(128)} %copy-done.46) | copy-start | bytes 1540
  501.8 36.5 %copy-start.37 = (f32[1024]{0:T(1024)S(1)}, f32[1024]{0:T(1024)}, u32[]{:S(2)}) copy-start(f32[1024]{0:T(1024)} %get-tuple-element.188) | copy-start | bytes 12292
  501.8 108.0 %copy-start.3 = (bf16[128,1024]{1,0:T(8,128)(2,1)S(1)}, bf16[128,1024]{1,0:T(8,128)(2,1)}, u32[]{:S(2)}) copy-start(bf16[128,1024]{1,0:T(8,128)(2,1)} %reduce-scatter.5.cloned.1.call-done) | copy-start | bytes 786436
  501.9 108.0 %copy-start.10 = (bf16[128,1024]{1,0:T(8,128)(2,1)S(1)}, bf16[128,1024]{1,0:T(8,128)(2,1)}, u32[]{:S(2)}) copy-start(bf16[128,1024]{1,0:T(8,128)(2,1)} %reduce-scatter.9.cloned.1.call-done) | copy-start | bytes 786436
  501.9 108.0 %copy-start.12 = (bf16[128,1024]{1,0:T(8,128)(2,1)S(1)}, bf16[128,1024]{1,0:T(8,128)(2,1)}, u32[]{:S(2)}) copy-start(bf16[128,1024]{1,0:T(8,128)(2,1)} %param.19) | copy-start | bytes 786436
  501.9 108.0 %copy-start.33 = (f32[1024]{0:T(1024)S(1)}, f32[1024]{0:T(1024)}, u32[]{:S(2)}) copy-start(f32[1024]{0:T(1024)} %param.18) | copy-start | bytes 12292
  501.9 108.0 %copy-start.40 = (f32[128]{0:T(128)S(1)}, f32[128]{0:T(128)}, u32[]{:S(2)}) copy-start(f32[128]{0:T(128)} %copy-done.38) | copy-start | bytes 1540
  501.9 108.0 %copy-start.43 = (f32[128]{0:T(128)S(1)}, f32[128]{0:T(128)}, u32[]{:S(2)}) copy-start(f32[128]{0:T(128)} %copy-done.41) | copy-start | bytes 1540
  501.9 108.0 %copy-start.49 = (f32[128]{0:T(128)S(1)}, f32[128]{0:T(128)}, u32[]{:S(2)}) copy-start(f32[128]{0:T(128)} %copy-done.48) | copy-start | bytes 1540
  501.9 108.0 %copy-start.51 = (f32[128]{0:T(128)S(1)}, f32[128]{0:T(128)}, u32[]{:S(2)}) copy-start(f32[128]{0:T(128)} %copy-done.50) | copy-start | bytes 1540
  (5 other events, 4.1 us)
Sparse Core Ops, SparseCore 0:
  11.6 39.4 all-gather.4
  74.5 41.8 reduce-scatter.4
  121.2 40.1 all-gather.6
  162.9 40.7 all-gather.8
  216.1 42.0 reduce-scatter.8
  262.2 40.1 all-gather.10
  340.9 154.7 all-reduce.3
  498.1 38.9 reduce-scatter.10
  539.5 41.8 reduce-scatter.6
where the time goes:
time: 620 us; the launch traced here: 619 us
  waiting for transfers between devices  414 us (67%)
  blocking collectives  71.4 us (12%)
  matrix products  49.2 us (8%)
  other arithmetic  35.8 us (6%)
  local copies, waits for them, and re-layouts  32.9 us (5%)
  between operations  14.6 us (2%)
    psum x1, waiting for transfers between devices, local(): lax.psum(attn_in_grad.astype(jnp.bfloat16), 'dp').astype(jnp.float32)  147 us
    psum x1, blocking collectives, local(): lax.psum((first_gain, second_gain), ('dp', 'tensor'))  71.4 us
    reduce_scatter x1, waiting for transfers between devices, local(): lax.psum_scatter((jnp.einsum('tf,df->td', gate_grad, mlp_in[0], preferred...  42.1 us
    reduce_scatter x1, waiting for transfers between devices, local(): lax.psum_scatter(jnp.dot(piece, out_weight, preferred_element_type=jnp.fl...  42 us
    all_gather x1, waiting for transfers between devices, local(): second_all = lax.all_gather(second_hidden, 'tensor', axis=0, tiled=True)  39.6 us
    all_gather x1, waiting for transfers between devices, local(): upstream_all = lax.all_gather(cotangent, 'tensor', axis=0, tiled=True)  38.7 us
    all_gather x1, waiting for transfers between devices, local(): first_all = lax.all_gather(first_hidden, 'tensor', axis=0, tiled=True)  37.5 us
    reduce_scatter x1, waiting for transfers between devices, local(): lax.psum_scatter(jnp.einsum('tc,dc->td', piece, proj_weight, preferred_el...  33.3 us
  transfers between devices with their start and end apart: 9, of which 8 were waited for; matrix products, arithmetic and copies ran while one was open for 4% of the time, Pallas kernels for 0%

commit v1 on v0

v1 whole, which is shorter than its diff:
```python
import jax
import jax.numpy as jnp
import numpy as np
from jax import lax
from jax.experimental import pallas as pl
from jax.experimental.pallas import tpu as pltpu
from jax.sharding import PartitionSpec as P

MESH = pl.DeviceIdType.MESH
BF = jnp.bfloat16
F32 = jnp.float32
EPS = 1e-05
THETA = 160000.0
T = 1024
D = 1024
B = 128
FF = 328
FP = 384
FR = 336


def tables():
    places = np.arange(T, dtype=np.float32)
    frequency = (THETA ** (-np.arange(0, 64, 2, dtype=np.float32) / 64)).astype(np.float32)
    angles = places[:, None] * frequency[None, :]
    cosine, sine = np.cos(angles), np.sin(angles)
    cosine = np.concatenate([cosine, cosine] * 2, -1)
    signed = np.concatenate([-sine, sine] * 2, -1)
    order = np.concatenate([np.arange(B) + ((j % 2) * 4 + j // 2) * B for j in range(8)])
    return cosine[order].astype(np.float32), signed[order].astype(np.float32)


def nn(a, b):
    return jnp.dot(a, b, preferred_element_type=F32)


def nt(a, b):
    return lax.dot_general(a, b, (((1,), (1,)), ((), ())), preferred_element_type=F32)


def swap_halves(u):
    lane = lax.broadcasted_iota(jnp.int32, u.shape, 1)
    return jnp.where((lane % 64) < 32, pltpu.roll(u, 96, 1), pltpu.roll(u, 32, 1))


def norm(v):
    centred = v - jnp.mean(v, -1, keepdims=True)
    inverse = lax.rsqrt(jnp.mean(centred * centred, -1, keepdims=True) + EPS)
    return centred * inverse, inverse


def norm_back(gradient, xhat, inverse, gain):
    e = gradient * gain
    dx = inverse * (
        e - jnp.mean(e, -1, keepdims=True) - xhat * jnp.mean(e * xhat, -1, keepdims=True)
    )
    return dx, jnp.sum(gradient * xhat, 0, keepdims=True)


def rows(start, size):
    return pl.ds(pl.multiple_of(start, 16), size)


def cols(start, size):
    return pl.ds(pl.multiple_of(start, 128), size)


def remote(src, dst, ssem, rsem, dev):
    return pltpu.make_async_remote_copy(
        src_ref=src, dst_ref=dst, send_sem=ssem, recv_sem=rsem, device_id=dev, device_id_type=MESH
    )


class Place:
    def __init__(self):
        dp, tensor = lax.axis_index("dp"), lax.axis_index("tensor")
        self.dp, self.tensor = dp, tensor
        self.c = dp % 2
        self.xlo, self.y = tensor // 4, tensor % 4
        self.z = dp // 4
        self.x = ((dp // 2) % 2) * 2 + self.xlo
        self.me = 2 * self.y + self.c
        self.mover = self.c != self.xlo
        self.right, self.left = (self.y + 1) % 4, (self.y + 3) % 4
        self.opp = (self.y + 2) % 4

    def team(self, core, y):
        return {"dp": self.dp - self.c + core, "tensor": self.xlo * 4 + y}

    def plane(self, x, z, core=None):
        core = self.c if core is None else core
        return {"dp": z * 4 + (x // 2) * 2 + core, "tensor": (x % 2) * 4 + self.y}

    def partner(self):
        return {"dp": self.dp - self.c + self.xlo, "tensor": self.c * 4 + self.y}


class Gather:
    def __init__(self, place, buf, ssem, rsem):
        self.p, self.buf, self.ssem, self.rsem = place, buf, ssem, rsem

    def msg(self, i):
        p = self.p
        me, lt, rt, op = p.me, 2 * p.left + p.c, 2 * p.right + p.c, 2 * p.opp + p.c
        right, left = p.team(p.c, p.right), p.team(p.c, p.left)
        sib = p.team(1 - p.c, p.y)
        block, first, size, dev = (
            (me, 0, 64, right),
            (me, 64, 64, left),
            (me, 64, 64, right),
            (me, 0, 64, left),
            (me, 0, 128, sib),
            (lt, 0, 64, right),
            (rt, 64, 64, left),
            (lt, 0, 128, sib),
            (rt, 0, 128, sib),
            (op, 0, 64, sib),
            (op, 64, 64, sib),
        )[i]
        ref = self.buf.at[rows(block * B + first, size)]
        return remote(ref, ref, self.ssem.at[i], self.rsem.at[i], dev)

    def start(self):
        for i in range(5):
            self.msg(i).start()

    def first(self):
        self.msg(4).wait_recv()

    def second(self):
        self.msg(0).wait_recv()
        self.msg(5).start()
        self.msg(1).wait_recv()
        self.msg(6).start()
        self.msg(2).wait_recv()
        self.msg(7).start()
        self.msg(3).wait_recv()
        self.msg(8).start()

    def third(self):
        self.msg(5).wait_recv()
        self.msg(9).start()
        self.msg(6).wait_recv()
        self.msg(10).start()

    def left_in(self):
        self.msg(7).wait_recv()

    def right_in(self):
        self.msg(8).wait_recv()

    def opp_in(self):
        self.msg(9).wait_recv()
        self.msg(10).wait_recv()

    def sent(self):
        for i in range(11):
            self.msg(i).wait_send()

    def rest(self):
        self.left_in()
        self.right_in()
        self.opp_in()
        self.sent()

    def steps(self, body):
        p = self.p

        @pl.loop(0, 4)
        def _(step):
            @pl.when(step == 0)
            def _():
                self.first()

            @pl.when(step == 1)
            def _():
                self.second()
                self.left_in()

            @pl.when(step == 2)
            def _():
                self.right_in()

            @pl.when(step == 3)
            def _():
                self.third()
                self.opp_in()

            off = jnp.where(step == 0, 0, jnp.where(step == 1, 3, jnp.where(step == 2, 1, 2)))
            body((p.y + off) % 4)

        self.sent()


class Scatter:
    def __init__(self, place, part, got, held, top, bottom, from_left, from_right, ssem, rsem):
        self.p = place
        self.part, self.got, self.held = part, got, held
        self.top, self.bottom = top, bottom
        self.from_left, self.from_right = from_left, from_right
        self.ssem, self.rsem = ssem, rsem

    def off(self, step):
        return jnp.where(step == 0, 2, jnp.where(step == 1, 1, jnp.where(step == 2, 3, 0)))

    def sib(self, step):
        p = self.p
        yy = (p.y + self.off(step)) % 4
        return remote(
            self.part.at[rows((2 * yy + 1 - p.c) * B, B)],
            self.got.at[rows(yy * B, B)],
            self.ssem.at[step],
            self.rsem.at[step],
            p.team(1 - p.c, p.y),
        )

    def msg(self, i):
        p = self.p
        right, left = p.team(p.c, p.right), p.team(p.c, p.left)
        block, first, dst, dev = (
            (p.opp, 0, self.top, right),
            (p.opp, 64, self.bottom, left),
            (p.right, 64, self.from_left.at[rows(64, 64)], right),
            (p.right, 0, self.from_left.at[rows(0, 64)], right),
            (p.left, 0, self.from_right.at[rows(0, 64)], left),
            (p.left, 64, self.from_right.at[rows(64, 64)], left),
        )[i]
        return remote(
            self.held.at[rows(block * B + first, 64)], dst, self.ssem.at[4 + i], self.rsem.at[4 + i], dev
        )

    def phase(self, compute):
        p = self.p

        @pl.loop(0, 4)
        def _(step):
            yy = (p.y + self.off(step)) % 4
            self.part[rows(yy * 256, 256), :] = compute(yy).astype(BF)
            self.sib(step).start()

    def pair_sum(self, yy):
        own = self.part[rows((2 * yy + self.p.c) * B, B), :].astype(F32)
        return own + self.got[rows(yy * B, B), :].astype(F32)

    def step0(self):
        p = self.p
        self.sib(0).wait_recv()
        self.held[rows(p.opp * B, B), :] = self.pair_sum(p.opp).astype(BF)
        self.msg(0).start()
        self.msg(1).start()

    def step1(self):
        p = self.p
        self.sib(1).wait_recv()
        total = self.pair_sum(p.right)
        self.held[rows(p.right * B + 64, 64), :] = total[64:].astype(BF)
        self.msg(2).start()
        self.sib(2).wait_recv()
        total2 = self.pair_sum(p.left)
        self.held[rows(p.left * B, 64), :] = total2[:64].astype(BF)
        self.msg(4).start()
        self.msg(0).wait_recv()
        self.held[rows(p.right * B, 64), :] = (total[:64] + self.top[...].astype(F32)).astype(BF)
        self.msg(3).start()
        self.msg(1).wait_recv()
        self.held[rows(p.left * B + 64, 64), :] = (total2[64:] + self.bottom[...].astype(F32)).astype(BF)
        self.msg(5).start()

    def step2(self):
        p = self.p
        self.sib(3).wait_recv()
        total = self.pair_sum(p.y)
        for i in range(2, 6):
            self.msg(i).wait_recv()
        total = total + self.from_left[...].astype(F32) + self.from_right[...].astype(F32)
        for i in range(4):
            self.sib(i).wait_send()
        for i in range(6):
            self.msg(i).wait_send()
        return total


class Sums:
    def __init__(self, place, full, slots, mine, out, size, ssem, rsem, bsem, esem):
        self.p = place
        self.full, self.slots, self.mine, self.out = full, slots, mine, out
        self.size = size
        self.ssem, self.rsem, self.bsem, self.esem = ssem, rsem, bsem, esem

    def peer(self, k):
        return (self.p.x + k % 4) % 4, (self.p.z + k // 4) % 4

    def spread_msg(self, k):
        x, z = self.peer(k)
        return remote(
            self.full.at[rows((z * 4 + x) * self.size, self.size)],
            self.slots.at[rows(k * self.size, self.size)],
            self.ssem.at[k],
            self.rsem.at[k],
            self.p.plane(x, z),
        )

    def spread(self):
        @pl.loop(1, 16)
        def _(k):
            self.spread_msg(k).start()

    def add(self):
        p, size = self.p, self.size

        @pl.loop(1, 16)
        def _(k):
            self.spread_msg(k).wait_recv()

        @pl.loop(0, size // 16)
        def _(r):
            total = self.full[rows((p.z * 4 + p.x) * size + r * 16, 16), :].astype(F32)
            for k in range(1, 16):
                total = total + self.slots[rows(k * size + r * 16, 16), :].astype(F32)
            self.mine[rows(r * 16, 16), :] = total.astype(BF)

        @pl.loop(1, 16)
        def _(k):
            self.spread_msg(k).wait_send()

    def return_msg(self, k):
        p = self.p
        x, z = self.peer(k)
        return remote(
            self.mine,
            self.out.at[rows((p.z * 4 + p.x) * self.size, self.size)],
            self.bsem.at[k],
            self.bsem.at[16 + k],
            p.plane(x, z),
        )

    def goes(self, k):
        return ((self.p.x + k % 4) % 2 == self.p.c) & (k != 0)

    def give(self):
        p = self.p

        @pl.loop(0, 16)
        def _(k):
            @pl.when(self.goes(k))
            def _():
                self.return_msg(k).start()

        @pl.when(jnp.logical_not(p.mover))
        def _():
            self.out[rows((p.z * 4 + p.x) * self.size, self.size), :] = self.mine[...]

    def forward(self):
        p = self.p
        return remote(self.out, self.out, self.esem.at[0], self.esem.at[1], p.team(1 - p.c, p.y))

    def take(self):
        p = self.p

        @pl.when(jnp.logical_not(p.mover))
        def _():
            @pl.loop(1, 16)
            def _(k):
                self.return_msg(k).wait_recv()

            self.forward().start()

    def finish(self):
        p = self.p

        @pl.when(p.mover)
        def _():
            self.forward().wait_recv()

        @pl.when(jnp.logical_not(p.mover))
        def _():
            self.forward().wait_send()

        @pl.loop(0, 16)
        def _(k):
            @pl.when(self.goes(k))
            def _():
                self.return_msg(k).wait_send()


class Gain:
    def __init__(self, place, team_buf, plane_buf, sems):
        self.p, self.team_buf, self.plane_buf, self.sems = place, team_buf, plane_buf, sems

    def team_msg(self, k):
        p = self.p
        j = (p.me + k) % 8
        ref = self.team_buf.at[p.me]
        return remote(ref, ref, self.sems.at[0, k], self.sems.at[1, k], p.team(j % 2, j // 2))

    def plane_msg(self, k):
        p = self.p
        x, z = (p.x + k % 4) % 4, (p.z + k // 4) % 4
        ref = self.plane_buf.at[p.z * 4 + p.x]
        return remote(ref, ref, self.sems.at[2, k], self.sems.at[3, k], p.plane(x, z))

    def start(self, value):
        self.team_buf[self.p.me] = value

        @pl.loop(1, 8)
        def _(k):
            self.team_msg(k).start()

    def middle(self):
        @pl.loop(1, 8)
        def _(k):
            self.team_msg(k).wait_recv()

        self.plane_buf[self.p.z * 4 + self.p.x] = jnp.sum(self.team_buf[...], 0)

        @pl.loop(1, 16)
        def _(k):
            self.plane_msg(k).start()

        @pl.loop(1, 8)
        def _(k):
            self.team_msg(k).wait_send()

    def end(self):
        @pl.loop(1, 16)
        def _(k):
            self.plane_msg(k).wait_recv()

        total = jnp.sum(self.plane_buf[...], 0)

        @pl.loop(1, 16)
        def _(k):
            self.plane_msg(k).wait_send()

        return total


class Swap:
    def __init__(self, place, src, dst, sems, there=None):
        self.p, self.src, self.dst, self.sems = place, src, dst, sems
        self.there = dst if there is None else there

    def far(self):
        return remote(self.src, self.there, self.sems.at[0], self.sems.at[1], self.p.partner())

    def near(self):
        return pltpu.make_async_copy(self.src, self.dst, self.sems.at[2])

    def start(self):
        pl.when(self.p.mover)(lambda: self.far().start())
        pl.when(jnp.logical_not(self.p.mover))(lambda: self.near().start())

    def wait(self):
        pl.when(self.p.mover)(lambda: self.far().wait())
        pl.when(jnp.logical_not(self.p.mover))(lambda: self.near().wait())


class Fetch:
    def __init__(self, place, src, dst, halves, sems, there=None):
        self.p, self.src, self.dst, self.halves, self.sems = place, src, dst, halves, sems
        self.there = dst if there is None else there

    def far(self, i):
        p = self.p
        x = (p.x + (1, 3)[i]) % 4
        part = self.halves[i]
        return remote(
            self.src.at[part],
            self.there.at[part],
            self.sems.at[i],
            self.sems.at[2 + i],
            p.plane(x, p.z, p.xlo),
        )

    def near(self):
        return pltpu.make_async_copy(self.src, self.dst, self.sems.at[4])

    def start(self):
        @pl.when(self.p.mover)
        def _():
            self.far(0).start()
            self.far(1).start()

        pl.when(jnp.logical_not(self.p.mover))(lambda: self.near().start())

    def wait(self):
        @pl.when(self.p.mover)
        def _():
            self.far(0).wait()
            self.far(1).wait()

        pl.when(jnp.logical_not(self.p.mover))(lambda: self.near().wait())


class Exchange:
    def __init__(self, place, src_of, dst, ssem, rsem):
        self.p, self.src_of, self.dst = place, src_of, dst
        self.ssem, self.rsem = ssem, rsem

    def msg(self, k):
        p = self.p
        j = (p.me + k) % 8
        return remote(
            self.src_of(j), self.dst, self.ssem.at[k], self.rsem.at[k], p.team(j % 2, j // 2)
        )

    def start(self):
        @pl.loop(1, 8)
        def _(k):
            self.msg(k).start()

    def wait(self):
        @pl.loop(1, 8)
        def _(k):
            self.msg(k).wait_recv()

        @pl.loop(1, 8)
        def _(k):
            self.msg(k).wait_send()


SCRATCH = dict(
    xb=((B, D), BF),
    cotb=((T, D), BF),
    w=((D, 384), BF),
    wo=((T, D), BF),
    wg=((2, D, FP), BF),
    wm=((FP, D), BF),
    h1=((T, D), BF),
    h2=((T, D), BF),
    gb=((T, D), BF),
    xhat1=((B, D), F32),
    inv1=((B, 1), F32),
    y1=((B, D), F32),
    xhat2=((B, D), F32),
    inv2=((B, 1), F32),
    gy=((B, D), F32),
    q=((T, B), BF),
    qt=((2, B, T), BF),
    k=((T, B), BF),
    kt=((B, T), BF),
    v=((T, B), BF),
    vt=((B, T), BF),
    pt=((2, T, T), BF),
    ot=((B, T), F32),
    o=((T, B), BF),
    orow=((B, D), BF),
    dorow=((B, D), BF),
    dob=((T, B), BF),
    dot=((2, B, T), BF),
    dsum=((2, 1, T), F32),
    ds=((T, T), BF),
    dqt=((B, T), F32),
    dk=((T, B), F32),
    dv=((T, B), F32),
    dqkv=((T, 384), BF),
    dqkvt=((384, T), BF),
    m=((T, FP), BF),
    da=((T, FP), BF),
    db=((T, FP), BF),
    mt=((FP, T), BF),
    dat=((FP, T), BF),
    dbt=((FP, T), BF),
    gm=((1024, D), BF),
    gm_slots=((1024, D), BF),
    gm_mine=((64, D), BF),
    gm_out=((1024, D), BF),
    ga=((512, D), BF),
    ga_slots=((512, D), BF),
    ga_mine=((32, D), BF),
    ga_out=((512, D), BF),
    g1t=((8, 1, D), F32),
    g1p=((16, 1, D), F32),
    g2t=((8, 1, D), F32),
    g2p=((16, 1, D), F32),
    lo_here=((B, D), BF),
    lo_out=((B, D), BF),
    tg_here=((B, D), BF),
    tg_out=((B, D), BF),
)
for _name in ("r2", "ro", "r1"):
    SCRATCH.update(
        {
            _name + "_part": ((T, D), BF),
            _name + "_got": ((512, D), BF),
            _name + "_held": ((512, D), BF),
            _name + "_top": ((64, D), BF),
            _name + "_bottom": ((64, D), BF),
            _name + "_left": ((B, D), BF),
            _name + "_right": ((B, D), BF),
        }
    )
SEMS = dict(
    ag_h1=(2, 11), ag_wo=(2, 11), ag_cot=(2, 11), ag_h2=(2, 11), ag_gb=(2, 11),
    rs_r2=(2, 10), rs_ro=(2, 10), rs_r1=(2, 10),
    sm=(2, 16), sm_back=(32,), sm_fwd=(2,),
    sa=(2, 16), sa_back=(32,), sa_fwd=(2,),
    g1=(4, 16), g2=(4, 16),
    sw_x=(3,), sw_cot=(3,), sw_lo=(3,), sw_tg=(3,),
    f_w=(5,), f_wo=(5,), f_wg=(5,), f_wm=(5,),
    x_o=(2, 8), x_do=(2, 8), outs=(4,),
)


def kernel(
    tok, cot, win, wout, wgate, wmix, gain1, gain2, cosine, signed,
    lo_ref, tg_ref, gm_ref, ga_ref, gains_ref, *scratch
):
    names = list(SCRATCH) + ["s_" + n for n in SEMS]
    s = dict(zip(names, scratch, strict=True))
    p = Place()

    class R:
        pass

    r = R()
    r.__dict__.update(s)

    barrier = pltpu.get_barrier_semaphore()

    @pl.loop(1, 8)
    def _(k):
        j = (p.me + k) % 8
        pl.semaphore_signal(barrier, inc=1, device_id=p.team(j % 2, j // 2), device_id_type=MESH)

    @pl.loop(1, 16)
    def _(k):
        dev = p.plane((p.x + k % 4) % 4, (p.z + k // 4) % 4)
        pl.semaphore_signal(barrier, inc=1, device_id=dev, device_id_type=MESH)

    for d in (1, 3):
        dev = p.plane((p.x + d) % 4, p.z, 1 - p.c)
        pl.semaphore_signal(barrier, inc=1, device_id=dev, device_id_type=MESH)
    pl.semaphore_wait(barrier, 24)

    def gather(buf, name):
        sem = s["s_ag_" + name]
        return Gather(p, buf, sem.at[0], sem.at[1])

    def scatter(name):
        parts = [s[name + "_" + n] for n in ("part", "got", "held", "top", "bottom", "left", "right")]
        sem = s["s_rs_" + name]
        return Scatter(p, *parts, sem.at[0], sem.at[1])

    own = rows(p.me * B, B)
    other = rows((2 * p.y + 1 - p.c) * B, B)
    own_cols = cols(p.me * B, B)

    sw_x = Swap(p, tok, r.xb, r.s_sw_x)
    f_w = Fetch(p, win, r.w, (pl.ds(0, 512), pl.ds(512, 512)), r.s_f_w)
    sw_x.start()
    f_w.start()
    sw_x.wait()

    xhat, inverse = norm(r.xb[...].astype(F32))
    r.xhat1[...] = xhat
    r.inv1[...] = inverse
    r.h1[own, :] = (xhat * gain1[...]).astype(BF)
    ag_h1 = gather(r.h1, "h1")
    ag_h1.start()

    f_wo = Fetch(p, wout, r.wo.at[own], (pl.ds(0, 64), pl.ds(64, 64)), r.s_f_wo, r.wo.at[other])
    sw_cot = Swap(p, cot, r.cotb.at[own], r.s_sw_cot, r.cotb.at[other])
    f_wo.start()
    sw_cot.start()
    r.qt[...] = jnp.zeros_like(r.qt)
    f_w.wait()

    def project(yy):
        at = rows(yy * 256, 256)
        lanes = cols(yy * 256, 256)
        u = nn(r.h1[at, :], r.w[...])
        co, si = cosine[at, :], signed[at, :]
        q = u[:, :128]
        q = (q * co + swap_halves(q) * si).astype(BF).astype(F32) * 0.125
        r.q[at, :] = q.astype(BF)
        qt = q.T.astype(BF)
        r.qt[0, 0:64, lanes] = qt[0:64]
        r.qt[1, 64:128, lanes] = qt[64:128]
        k = u[:, 128:256]
        k = k * co + swap_halves(k) * si
        r.k[at, :] = k.astype(BF)
        r.kt[:, lanes] = k.T.astype(BF)
        v = u[:, 256:]
        r.v[at, :] = v.astype(BF)
        r.vt[:, lanes] = v.T.astype(BF)

    ag_h1.steps(project)
    f_wg = Fetch(p, wgate, r.wg, (0, 1), r.s_f_wg)
    f_wm = Fetch(p, wmix, r.wm, (pl.ds(0, 192), pl.ds(192, 192)), r.s_f_wm)
    f_wg.start()
    f_wm.start()
    ag_wo = gather(r.wo, "wo")
    ag_cot = gather(r.cotb, "cot")
    f_wo.wait()
    ag_wo.start()

    @pl.loop(0, 8)
    def _(it):
        h, part = it // 4, it % 4
        lanes = cols(part * 256, 256)

        @pl.when(it == 2)
        def _():
            ag_wo.first()
            ag_wo.second()

        @pl.when(it == 4)
        def _():
            ag_wo.third()

        scores = nn(r.k[...], r.qt[h, :, lanes])
        powers = jnp.exp(scores - jnp.max(scores, 0, keepdims=True))
        probs = (powers * (1.0 / jnp.sum(powers, 0, keepdims=True))).astype(BF)
        r.pt[h, :, lanes] = probs
        half = rows(h * 64, 64)
        r.ot[half, lanes] = nn(r.vt[half, :], probs)

    r.o[...] = r.ot[...].T.astype(BF)
    x_o = Exchange(
        p, lambda j: r.o.at[rows(j * B, B)], r.orow.at[:, own_cols], r.s_x_o.at[0], r.s_x_o.at[1]
    )
    x_o.start()
    r.orow[:, own_cols] = r.o[own, :]
    ag_wo.rest()
    sw_cot.wait()
    ag_cot.start()
    x_o.wait()

    y1 = r.xb[...].astype(F32) + nn(r.orow[...], r.wo[...])
    r.y1[...] = y1
    xhat, inverse = norm(y1)
    r.xhat2[...] = xhat
    r.inv2[...] = inverse
    r.h2[own, :] = (xhat * gain2[...]).astype(BF)
    ag_h2 = gather(r.h2, "h2")
    ag_cot.first()
    ag_cot.second()
    ag_h2.start()
    ag_cot.third()
    ag_cot.rest()
    f_wg.wait()
    f_wm.wait()

    def mix(yy):
        at = rows(yy * 256, 256)
        lanes = cols(yy * 256, 256)
        h2 = r.h2[at, :]
        a = nn(h2, r.wg[0])
        b = nn(h2, r.wg[1])
        cdf = 0.5 * (1.0 + lax.erf(a * 0.7071067811865476))
        gelu = a * cdf
        slope = cdf + a * (jnp.exp(-0.5 * a * a) * 0.3989422804014327)
        m = gelu * b
        dm = nt(r.cotb[at, :], r.wm[...]).astype(BF).astype(F32)
        da = dm * b * slope
        db = dm * gelu
        r.m[at, :] = m.astype(BF)
        r.da[at, :] = da.astype(BF)
        r.db[at, :] = db.astype(BF)
        r.mt[:, lanes] = m.T.astype(BF)
        r.dat[:, lanes] = da.T.astype(BF)
        r.dbt[:, lanes] = db.T.astype(BF)

    ag_h2.steps(mix)

    def back_mix(yy):
        at = rows(yy * 256, 256)
        return nt(r.da[at, :], r.wg[0]) + nt(r.db[at, :], r.wg[1])

    rs_2 = scatter("r2")
    rs_2.phase(back_mix)
    rs_2.step0()

    def weight_grad(out, first, lhs, size, rhs):
        @pl.loop(0, 4)
        def _(i):
            lanes = cols(i * 256, 256)
            out[first : first + size, lanes] = nn(lhs[0:size, :], rhs[:, lanes]).astype(BF)

    weight_grad(r.gm, 0, r.mt, FR, r.cotb)
    rs_2.step1()
    weight_grad(r.gm, FR, r.dat, FR, r.h2)
    weight_grad(r.gm, 2 * FR, r.dbt, FR, r.h2)
    r.gm[3 * FR :, :] = jnp.zeros((1024 - 3 * FR, D), BF)
    dh2 = rs_2.step2()

    dx, dgain2 = norm_back(dh2, r.xhat2[...], r.inv2[...], gain2[...])
    gy = r.cotb[own, :].astype(F32) + dx
    r.gy[...] = gy
    r.gb[own, :] = gy.astype(BF)
    r.dorow[...] = nt(r.gb[own, :], r.wo[...]).astype(BF)
    x_do = Exchange(
        p, lambda j: r.dorow.at[:, cols(j * B, B)], r.dob.at[own], r.s_x_do.at[0], r.s_x_do.at[1]
    )
    x_do.start()
    r.dob[own, :] = r.dorow[:, own_cols]
    gain_2 = Gain(p, r.g2t, r.g2p, r.s_g2)
    gain_2.start(dgain2)
    sums_m = Sums(
        p, r.gm, r.gm_slots, r.gm_mine, r.gm_out, 64, r.s_sm.at[0], r.s_sm.at[1], r.s_sm_back, r.s_sm_fwd
    )
    sums_m.spread()
    rs_o = scatter("ro")
    rs_o.phase(lambda yy: nn(r.m[rows(yy * 256, 256), :], r.wm[...]))
    x_do.wait()
    ag_gb = gather(r.gb, "gb")
    ag_gb.start()
    rs_o.step0()

    dot = r.dob[...].astype(F32).T
    r.dot[...] = jnp.zeros_like(r.dot)
    r.dot[0, 0:64, :] = dot[0:64].astype(BF)
    r.dot[1, 64:128, :] = dot[64:128].astype(BF)
    prod = dot * r.ot[...]
    r.dsum[0] = jnp.sum(prod[0:64], 0, keepdims=True)
    r.dsum[1] = jnp.sum(prod[64:128], 0, keepdims=True)

    @pl.loop(0, 8)
    def _(it):
        h, part = it // 4, it % 4
        lanes = cols(part * 256, 256)

        @pl.when(it == 2)
        def _():
            rs_o.step1()
            gain_2.middle()

        @pl.when(it == 4)
        def _():
            ag_gb.first()
            ag_gb.second()

        @pl.when(it == 6)
        def _():
            ag_gb.third()

        dp = nn(r.v[...], r.dot[h, :, lanes])
        ds = (r.pt[h, :, lanes].astype(F32) * (dp - r.dsum[h, :, lanes])).astype(BF)
        r.ds[:, lanes] = ds
        half = rows(h * 64, 64)
        r.dqt[half, lanes] = nn(r.kt[half, :], ds)

        @pl.when(part == 3)
        def _():
            @pl.loop(0, 4)
            def _(i):
                at = rows(i * 256, 256)
                lane = lax.broadcasted_iota(jnp.int32, (256, B), 1)
                keep = (lane // 64) == h
                r.dk[at, :] = jnp.where(keep, nn(r.ds[at, :], r.q[...]), r.dk[at, :])
                r.dv[at, :] = jnp.where(keep, nn(r.pt[h, at, :], r.dob[...]), r.dv[at, :])

    @pl.loop(0, 4)
    def _(i):
        at = rows(i * 256, 256)
        lanes = cols(i * 256, 256)
        co, si = cosine[at, :], signed[at, :]
        dq = r.dqt[:, lanes].T * 0.125
        dq = dq * co - swap_halves(dq) * si
        dk = r.dk[at, :]
        dk = dk * co - swap_halves(dk) * si
        dv = r.dv[at, :]
        r.dqkv[at, 0:128] = dq.astype(BF)
        r.dqkv[at, 128:256] = dk.astype(BF)
        r.dqkv[at, 256:384] = dv.astype(BF)
        r.dqkvt[0:128, lanes] = dq.T.astype(BF)
        r.dqkvt[128:256, lanes] = dk.T.astype(BF)
        r.dqkvt[256:384, lanes] = dv.T.astype(BF)

    rs_1 = scatter("r1")
    rs_1.phase(lambda yy: nt(r.dqkv[rows(yy * 256, 256), :], r.w[...]))
    rs_1.step0()
    weight_grad(r.ga, 0, r.dqkvt, 384, r.h1)
    ag_gb.rest()

    @pl.loop(0, 4)
    def _(i):
        lanes = cols(i * 256, 256)
        r.ga[384:512, lanes] = nn(r.ot[...].astype(BF), r.gb[:, lanes]).astype(BF)

    sums_a = Sums(
        p, r.ga, r.ga_slots, r.ga_mine, r.ga_out, 32, r.s_sa.at[0], r.s_sa.at[1], r.s_sa_back, r.s_sa_fwd
    )
    sums_a.spread()
    rs_1.step1()
    sums_m.add()
    sums_m.give()
    r.lo_here[...] = (r.y1[...] + rs_o.step2()).astype(BF)
    sw_lo = Swap(p, r.lo_here, r.lo_out, r.s_sw_lo)
    sw_lo.start()
    dh1 = rs_1.step2()
    dx, dgain1 = norm_back(dh1, r.xhat1[...], r.inv1[...], gain1[...])
    gain_1 = Gain(p, r.g1t, r.g1p, r.s_g1)
    gain_1.start(dgain1)
    r.tg_here[...] = (r.gy[...] + dx).astype(BF)
    sw_tg = Swap(p, r.tg_here, r.tg_out, r.s_sw_tg)
    sw_tg.start()
    sums_a.add()
    sums_a.give()
    gain_1.middle()
    sums_m.take()
    sw_lo.wait()
    lo_copy = pltpu.make_async_copy(r.lo_out, lo_ref, r.s_outs.at[0])
    lo_copy.start()
    sw_tg.wait()
    tg_copy = pltpu.make_async_copy(r.tg_out, tg_ref, r.s_outs.at[1])
    tg_copy.start()
    gains_ref[1:2, :] = gain_2.end()
    sums_m.finish()
    gm_copy = pltpu.make_async_copy(r.gm_out, gm_ref, r.s_outs.at[2])
    gm_copy.start()
    gains_ref[0:1, :] = gain_1.end()
    sums_a.take()
    sums_a.finish()
    ga_copy = pltpu.make_async_copy(r.ga_out, ga_ref, r.s_outs.at[3])
    ga_copy.start()
    lo_copy.wait()
    tg_copy.wait()
    gm_copy.wait()
    ga_copy.wait()


def local(tokens, attn_in, attn_out, mlp_in, mlp_out, norm_first, norm_second, cotangent):
    cosine, signed = tables()
    any_space = pl.BlockSpec(memory_space=pl.ANY)
    vmem = pl.BlockSpec(memory_space=pltpu.VMEM)
    lo, tg, gm, ga, gains = pl.pallas_call(
        kernel,
        out_shape=(
            jax.ShapeDtypeStruct((B, D), BF),
            jax.ShapeDtypeStruct((B, D), BF),
            jax.ShapeDtypeStruct((1024, D), BF),
            jax.ShapeDtypeStruct((512, D), BF),
            jax.ShapeDtypeStruct((2, D), F32),
        ),
        in_specs=[any_space] * 6 + [vmem] * 4,
        out_specs=(any_space, any_space, any_space, any_space, vmem),
        scratch_shapes=[pltpu.VMEM(shape, kind) for shape, kind in SCRATCH.values()]
        + [pltpu.SemaphoreType.DMA(shape) for shape in SEMS.values()],
        compiler_params=pltpu.CompilerParams(
            collective_id=0, has_side_effects=True, vmem_limit_bytes=63 * 1024 * 1024
        ),
    )(
        tokens,
        cotangent,
        attn_in.reshape(D, 384),
        attn_out.reshape(B, D),
        jnp.pad(mlp_in, ((0, 0), (0, 0), (0, FP - FF))),
        jnp.pad(mlp_out, ((0, FP - FF), (0, 0))),
        norm_first.reshape(1, D),
        norm_second.reshape(1, D),
        jnp.asarray(cosine),
        jnp.asarray(signed),
    )
    attn_in_grad = ga[:384].astype(F32).T.reshape(D, 3, 2, 64)
    attn_out_grad = ga[384:].astype(F32).reshape(2, 64, D)
    mlp_out_grad = gm[:FF].astype(F32)
    mlp_in_grad = jnp.stack(
        [gm[FR : FR + FF].astype(F32).T, gm[2 * FR : 2 * FR + FF].astype(F32).T]
    )
    return (
        lo,
        tg.astype(F32),
        attn_in_grad,
        attn_out_grad,
        mlp_in_grad,
        mlp_out_grad,
        gains[0],
        gains[1],
    )


def solution(mesh):
    placed = (
        P(("dp", "tensor"), None),
        P(None, None, "tensor", None),
        P("tensor", None, None),
        P(None, None, "tensor"),
        P("tensor", None),
        P(),
        P(),
        P(("dp", "tensor"), None),
    )
    return jax.shard_map(
        local,
        mesh=mesh,
        in_specs=placed,
        out_specs=(
            P(("dp", "tensor"), None),
            P(("dp", "tensor"), None),
            P(None, None, "tensor", None),
            P("tensor", None, None),
            P(None, None, "tensor"),
            P("tensor", None),
            P(),
            P(),
        ),
        check_vma=False,
    )
```

time: 620 us -> 178 us (0.29)
  waiting for transfers between devices: 414 us -> 0 us
  Pallas kernels: 0 us -> 163 us
  blocking collectives: 71.4 us -> 0 us
  matrix products: 49.2 us -> 0 us
  other arithmetic: 35.8 us -> 7.53 us
  local copies, waits for them, and re-layouts: 32.9 us -> 6.62 us
  between operations: 14.6 us -> 0.67 us
    pallas_call x0 -> x1, Pallas kernels: none -> 163 us  [local(): pl.pallas_call(kernel, out_shape=(jax.ShapeDtypeStruct((B, D), BF), jax.S...]
    all_gather x4 -> x0, waiting for transfers between devices: 148 us -> none  [the longest x1 39.6 us: local(): second_all = lax.all_gather(second_hidden, 'tensor', axis=0, tiled=True)]
    psum x1 -> x0, waiting for transfers between devices: 147 us -> none  [local(): lax.psum(attn_in_grad.astype(jnp.bfloat16), 'dp').astype(jnp.float32)]
    reduce_scatter x4 -> x0, waiting for transfers between devices: 117 us -> none  [the longest x1 42.1 us: local(): lax.psum_scatter((jnp.einsum('tf,df->td', gate_grad, mlp_in[0], preferred...]
    psum x1 -> x0, blocking collectives: 71.4 us -> none  [local(): lax.psum((first_gain, second_gain), ('dp', 'tensor'))]
    dot_general x29 -> x0, matrix products: 49.2 us -> none  [the longest x1 5.83 us: local(): jnp.einsum('td,fd->tf', upstream_all, mlp_out, preferred_element_type=jnp...]
    convert_element_type x11 -> x2, other arithmetic: 16.6 us -> 3.68 us  [the longest x1 2.84 us: local(): mlp_out_grad = gm[:FF].astype(F32)]
    dynamic_update_slice x4 -> x0, local copies, waits for them, and re-layouts: 12.1 us -> none  [sequence_forward(): outcome, log_sums = lax.map(block_forward, seq_queries.reshape(block_shape))]
  transfers between devices with their start and end apart: 9 -> 0, of which waited for: 8 -> 0; matrix products, arithmetic and copies ran while one was open for 4% -> 0% of each run, Pallas kernels for 0% -> 0%
where the time goes in v1:
time: 178 us
  Pallas kernels  163 us (92%)
  other arithmetic  7.53 us (4%)
  local copies, waits for them, and re-layouts  6.62 us (4%)
    pallas_call x1, Pallas kernels, local(): pl.pallas_call(kernel, out_shape=(jax.ShapeDtypeStruct((B, D), BF), jax.S...  163 us

profile of v1, /device:TPU:1, one launch (start us, length us, event | category | flops | bytes accessed | tf_op | source)
XLA Modules:
  0.0 177.7 jit_solution(8115876964693135098)
XLA Ops:
  0.6 1.8 %copy.20 = bf16[2,1024,328]{2,1,0:T(8,128)(2,1)S(1)} copy(bf16[2,1024,328]{1,2,0:T(8,128)(2,1)} %param.13) | data formatting | bytes 2686976 | tf_op args[3]
  2.5 0.0 copy-start.1
  2.5 1.3 pad.8.wgate
  3.8 0.0 copy-start.2
  3.8 0.0 copy-done.1
  3.8 1.2 copy.21.win
  5.0 0.0 copy-done.2
  5.0 1.0 pad.9.wmix
  5.9 162.8 %shard_map.161 = (bf16[128,1024]{1,0:T(8,128)(2,1)}, bf16[128,1024]{1,0:T(8,128)(2,1)}, bf16[1024,1024]{1,0:T(8,128)(2,1)}, bf16[512,1024]{1,0:T(8,128)(2,1)}, f32[2,1024]{1,0:T(2,128)}) custom-call(bf16[128,1024]{1,0:T(8,128)(2,1)} %tok.1, bf16[128,1024]{1,0:T(8,128)(2,1)} %cot.1, bf16[1024,384]{1,0:T(8,128)(2,1)} %copy.21.win, bf16[128,1024]{1,0:T(8,128)(2,1)} %bitcast.22, ...), custom_call_target="tpu_custom_call" | custom-call | tf_op jit(solution)/shard_map/pallas_call | solution.py:928
  168.8 2.8 %slice_convert_fusion.1 = (f32[328,1024]{1,0:T(8,128)}, bf16[1,1024,328]{1,2,0:T(8,128)(2,1)S(1)}, bf16[1,1024,328]{1,2,0:T(8,128)(2,1)S(1)}) fusion(bf16[1024,1024]{1,0:T(8,128)(2,1)} %get-tuple-element.16), kind=kLoop, calls=%fused_computation.2 | loop fusion | flops 335872 | bytes 4702208 | tf_op jit(solution)/shard_map/convert_element_type | solution.py:958
  171.6 0.0 copy-start
  171.6 1.7 maximum_convert_fusion
  173.3 0.0 copy-done
  173.3 0.0 copy-start.5
  173.3 0.0 copy-start.3
  173.3 1.3 slice_convert_fusion
  174.6 0.0 copy-start.4
  174.7 0.8 convert.8
  175.5 0.0 copy-done.5
  175.5 0.6 fusion
  176.1 0.0 copy-done.3
  176.1 0.8 convert_element_type.8
  177.0 0.0 copy-done.4
  177.0 0.7 copy.23
  (1 shorter events, 0.0 us)
Async XLA Ops:
  2.5 1.3 copy-start.1
  3.8 1.2 copy-start.2
  171.6 1.7 copy-start
  173.3 2.2 %copy-start.5 = (f32[2,1024]{1,0:T(2,128)S(1)}, f32[2,1024]{1,0:T(2,128)}, u32[]{:S(2)}) copy-start(f32[2,1024]{1,0:T(2,128)} %get-tuple-element.17) | copy-start | bytes 24580
  173.3 2.8 %copy-start.3 = (bf16[128,1024]{1,0:T(8,128)(2,1)S(1)}, bf16[128,1024]{1,0:T(8,128)(2,1)}, u32[]{:S(2)}) copy-start(bf16[128,1024]{1,0:T(8,128)(2,1)} %get-tuple-element.14) | copy-start | bytes 786436
  174.6 2.3 %copy-start.4 = (bf16[128,1024]{1,0:T(8,128)(2,1)S(1)}, bf16[128,1024]{1,0:T(8,128)(2,1)}, u32[]{:S(2)}) copy-start(bf16[128,1024]{1,0:T(8,128)(2,1)} %get-tuple-element.31) | copy-start | bytes 786436

commit v2 on v1

v2 whole, which is shorter than its diff:
```python
import jax
import jax.numpy as jnp
import numpy as np
from jax import lax
from jax.experimental import pallas as pl
from jax.experimental.pallas import tpu as pltpu
from jax.sharding import PartitionSpec as P

MESH = pl.DeviceIdType.MESH
BF = jnp.bfloat16
F32 = jnp.float32
EPS = 1e-05
THETA = 160000.0
T = 1024
D = 1024
B = 128
FF = 328
FR = 336
LOG2E = 1.4426950408889634


def tables():
    places = np.arange(T, dtype=np.float32)
    frequency = (THETA ** (-np.arange(0, 64, 2, dtype=np.float32) / 64)).astype(np.float32)
    angles = places[:, None] * frequency[None, :]
    cosine, sine = np.cos(angles), np.sin(angles)
    cosine = np.concatenate([cosine, cosine] * 2, -1)
    signed = np.concatenate([-sine, sine] * 2, -1)
    order = np.concatenate([np.arange(B) + ((j % 2) * 4 + j // 2) * B for j in range(8)])
    return cosine[order].astype(np.float32), signed[order].astype(np.float32)


def nn(a, b):
    return jnp.dot(a, b, preferred_element_type=F32)


def nt(a, b):
    return lax.dot_general(a, b, (((1,), (1,)), ((), ())), preferred_element_type=F32)


def pick(step, a, b, c, d):
    return jnp.where(step == 0, a, jnp.where(step == 1, b, jnp.where(step == 2, c, d)))


def swap_halves(u):
    lane = lax.broadcasted_iota(jnp.int32, u.shape, 1)
    return jnp.where((lane % 64) < 32, pltpu.roll(u, 96, 1), pltpu.roll(u, 32, 1))


def norm(v):
    centred = v - jnp.mean(v, -1, keepdims=True)
    inverse = lax.rsqrt(jnp.mean(centred * centred, -1, keepdims=True) + EPS)
    return centred * inverse, inverse


def norm_back(gradient, xhat, inverse, gain):
    e = gradient * gain
    dx = inverse * (
        e - jnp.mean(e, -1, keepdims=True) - xhat * jnp.mean(e * xhat, -1, keepdims=True)
    )
    return dx, jnp.sum(gradient * xhat, 0, keepdims=True)


def rows(start, size):
    return pl.ds(pl.multiple_of(start, 16), size)


def cols(start, size):
    return pl.ds(pl.multiple_of(start, 128), size)


def remote(src, dst, ssem, rsem, dev):
    return pltpu.make_async_remote_copy(
        src_ref=src, dst_ref=dst, send_sem=ssem, recv_sem=rsem, device_id=dev, device_id_type=MESH
    )


def drain(ref, sem):
    pltpu.make_async_copy(ref, ref, sem).wait()


class Place:
    def __init__(self):
        dp, tensor = lax.axis_index("dp"), lax.axis_index("tensor")
        self.dp, self.tensor = dp, tensor
        self.c = dp % 2
        self.xlo, self.y = tensor // 4, tensor % 4
        self.z = dp // 4
        self.x = ((dp // 2) % 2) * 2 + self.xlo
        self.me = 2 * self.y + self.c
        self.mover = self.c != self.xlo
        self.right, self.left = (self.y + 1) % 4, (self.y + 3) % 4
        self.opp = (self.y + 2) % 4

    def team(self, core, y):
        return {"dp": self.dp - self.c + core, "tensor": self.xlo * 4 + y}

    def plane(self, x, z, core=None):
        core = self.c if core is None else core
        return {"dp": z * 4 + (x // 2) * 2 + core, "tensor": (x % 2) * 4 + self.y}

    def partner(self):
        return {"dp": self.dp - self.c + self.xlo, "tensor": self.c * 4 + self.y}


class Gather:
    def __init__(self, place, buf, sems):
        self.p, self.buf, self.sems = place, buf, sems

    def msg(self, i):
        p = self.p
        me, lt, rt, op = p.me, 2 * p.left + p.c, 2 * p.right + p.c, 2 * p.opp + p.c
        right, left = p.team(p.c, p.right), p.team(p.c, p.left)
        sib = p.team(1 - p.c, p.y)
        block, first, size, dev = (
            (me, 0, 64, right),
            (me, 64, 64, left),
            (me, 64, 64, right),
            (me, 0, 64, left),
            (me, 0, 128, sib),
            (lt, 0, 64, right),
            (rt, 64, 64, left),
            (lt, 0, 128, sib),
            (rt, 0, 128, sib),
            (op, 0, 64, sib),
            (op, 64, 64, sib),
        )[i]
        ref = self.buf.at[rows(block * B + first, size)]
        return remote(ref, ref, self.sems.at[11], self.sems.at[i], dev)

    def start(self):
        for i in range(5):
            self.msg(i).start()

    def start_top(self):
        self.msg(0).start()
        self.msg(3).start()

    def start_bottom(self):
        self.msg(1).start()
        self.msg(2).start()
        self.msg(4).start()

    def first(self):
        self.msg(4).wait_recv()

    def second(self):
        self.msg(0).wait_recv()
        self.msg(5).start()
        self.msg(1).wait_recv()
        self.msg(6).start()
        self.msg(2).wait_recv()
        self.msg(7).start()
        self.msg(3).wait_recv()
        self.msg(8).start()

    def third(self):
        self.msg(5).wait_recv()
        self.msg(9).start()
        self.msg(6).wait_recv()
        self.msg(10).start()

    def left_in(self):
        self.msg(7).wait_recv()

    def right_in(self):
        self.msg(8).wait_recv()

    def opp_in(self):
        self.msg(9).wait_recv()
        self.msg(10).wait_recv()

    def sent(self):
        drain(self.buf.at[pl.ds(0, 896)], self.sems.at[11])

    def rest(self):
        self.left_in()
        self.right_in()
        self.opp_in()
        self.sent()

    def steps(self, body, hook=None, forwarded=False):
        p = self.p

        @pl.loop(0, 4)
        def _(step):
            @pl.when(step == 0)
            def _():
                self.first()

            @pl.when(step == 1)
            def _():
                if not forwarded:
                    self.second()
                self.left_in()

            @pl.when(step == 2)
            def _():
                self.right_in()

            @pl.when(step == 3)
            def _():
                self.third()
                self.opp_in()

            if hook is not None:
                hook(step)
            body((p.y + pick(step, 0, 3, 1, 2)) % 4)

        self.sent()


class Scatter:
    def __init__(self, place, part, got, held, top, bottom, from_left, from_right, sems):
        self.p = place
        self.part, self.got, self.held = part, got, held
        self.top, self.bottom = top, bottom
        self.from_left, self.from_right = from_left, from_right
        self.sems = sems

    def off(self, step):
        return pick(step, 2, 1, 3, 0)

    def sib(self, step):
        p = self.p
        yy = (p.y + self.off(step)) % 4
        return remote(
            self.part.at[rows((2 * yy + 1 - p.c) * B, B)],
            self.got.at[rows(yy * B, B)],
            self.sems.at[10],
            self.sems.at[step],
            p.team(1 - p.c, p.y),
        )

    def msg(self, i):
        p = self.p
        right, left = p.team(p.c, p.right), p.team(p.c, p.left)
        block, first, dst, dev = (
            (p.opp, 0, self.top, right),
            (p.opp, 64, self.bottom, left),
            (p.right, 64, self.from_left.at[rows(64, 64)], right),
            (p.right, 0, self.from_left.at[rows(0, 64)], right),
            (p.left, 0, self.from_right.at[rows(0, 64)], left),
            (p.left, 64, self.from_right.at[rows(64, 64)], left),
        )[i]
        return remote(
            self.held.at[rows(block * B + first, 64)], dst, self.sems.at[10], self.sems.at[4 + i], dev
        )

    def phase(self, compute, early=True, hook=None):
        p = self.p

        @pl.loop(0, 4)
        def _(step):
            yy = (p.y + self.off(step)) % 4
            self.part[rows(yy * 256, 256), :] = compute(yy).astype(BF)
            self.sib(step).start()
            if early:
                pl.when(step == 1)(self.step0)
                pl.when(step == 2)(self.step_right)
                pl.when(step == 3)(self.step_left)
            if hook is not None:
                hook(step)

    def pair_sum(self, yy):
        own = self.part[rows((2 * yy + self.p.c) * B, B), :].astype(F32)
        return own + self.got[rows(yy * B, B), :].astype(F32)

    def step0(self):
        p = self.p
        self.sib(0).wait_recv()
        self.held[rows(p.opp * B, B), :] = self.pair_sum(p.opp).astype(BF)
        self.msg(0).start()
        self.msg(1).start()

    def step_right(self):
        p = self.p
        self.sib(1).wait_recv()
        self.held[rows(p.right * B, B), :] = self.pair_sum(p.right).astype(BF)
        self.msg(2).start()

    def step_left(self):
        p = self.p
        self.sib(2).wait_recv()
        self.held[rows(p.left * B, B), :] = self.pair_sum(p.left).astype(BF)
        self.msg(4).start()

    def step1(self):
        p = self.p
        top, bottom = rows(p.right * B, 64), rows(p.left * B + 64, 64)
        self.msg(0).wait_recv()
        self.held[top, :] = (self.held[top, :].astype(F32) + self.top[...].astype(F32)).astype(BF)
        self.msg(3).start()
        self.msg(1).wait_recv()
        self.held[bottom, :] = (
            self.held[bottom, :].astype(F32) + self.bottom[...].astype(F32)
        ).astype(BF)
        self.msg(5).start()

    def step2(self):
        p = self.p
        self.sib(3).wait_recv()
        total = self.pair_sum(p.y)
        for i in range(2, 6):
            self.msg(i).wait_recv()
        total = total + self.from_left[...].astype(F32) + self.from_right[...].astype(F32)
        drain(self.part.at[pl.ds(0, 896)], self.sems.at[10])
        return total


class Sums:
    def __init__(self, place, full, slots, mine, out, sems):
        self.p = place
        self.full, self.slots, self.mine, self.out = full, slots, mine, out
        self.size = full.shape[0] // 2
        self.sems = sems

    def peer(self, k):
        return (self.p.x + k % 4) % 4, (self.p.z + k // 4) % 4

    def chunk(self, x, z):
        return rows((x % 2) * self.size, self.size), cols((z * 2 + x // 2) * B, B)

    def spread_msg(self, k):
        x, z = self.peer(k)
        return remote(
            self.full.at[self.chunk(x, z)],
            self.slots.at[k],
            self.sems.at[0],
            self.sems.at[1],
            self.p.plane(x, z),
        )

    def spread(self, off):
        @pl.loop(0, 4)
        def _(i):
            k = off * 4 + i

            @pl.when(k != 0)
            def _():
                self.spread_msg(k).start()

    def add(self):
        p, size = self.p, self.size

        drain(self.slots.at[pl.ds(1, 15)], self.sems.at[1])
        own_cols = cols((p.z * 2 + p.x // 2) * B, B)

        @pl.loop(0, size // 64)
        def _(r):
            total = self.full[rows((p.x % 2) * size + r * 64, 64), own_cols].astype(F32)
            for k in range(1, 16):
                total = total + self.slots[k, rows(r * 64, 64), :].astype(F32)
            self.mine[rows(r * 64, 64), :] = total.astype(BF)

    def return_msg(self, k):
        p = self.p
        x, z = self.peer(k)
        return remote(
            self.mine,
            self.out.at[self.chunk(p.x, p.z)],
            self.sems.at[2],
            self.sems.at[4 + k // 4],
            p.plane(x, z),
        )

    def goes(self, k):
        return ((self.p.x + k % 4) % 2 == self.p.c) & (k != 0)

    def give(self):
        p = self.p

        @pl.loop(0, 16)
        def _(k):
            @pl.when(self.goes(k))
            def _():
                self.return_msg(k).start()

        @pl.when(jnp.logical_not(p.mover))
        def _():
            at, lanes = self.chunk(p.x, p.z)
            self.out[at, lanes] = self.mine[...]

    def forward(self, i):
        p = self.p
        block = self.out.at[:, cols(((p.z + 4 - i) % 4) * 256, 256)]
        return remote(block, block, self.sems.at[3], self.sems.at[8 + i], p.team(1 - p.c, p.y))

    def take(self):
        p = self.p

        @pl.when(jnp.logical_not(p.mover))
        def _():
            for i in range(4):
                drain(self.slots.at[pl.ds(0, 4 if i else 3)], self.sems.at[4 + i])
                self.forward(i).start()

    def finish(self):
        p = self.p

        @pl.when(p.mover)
        def _():
            @pl.loop(0, 4)
            def _(i):
                self.forward(i).wait_recv()

            drain(self.slots.at[pl.ds(0, 8)], self.sems.at[2])

        @pl.when(jnp.logical_not(p.mover))
        def _():
            drain(self.out, self.sems.at[3])
            drain(self.slots.at[pl.ds(0, 7)], self.sems.at[2])

        drain(self.slots.at[pl.ds(1, 15)], self.sems.at[0])


class Gain:
    def __init__(self, place, team_buf, plane_buf, sems):
        self.p, self.team_buf, self.plane_buf, self.sems = place, team_buf, plane_buf, sems

    def start(self, value):
        p = self.p
        ref = self.team_buf.at[p.me]
        ref[...] = value

        @pl.loop(1, 8)
        def _(k):
            j = (p.me + k) % 8
            remote(ref, ref, self.sems.at[0], self.sems.at[1], p.team(j % 2, j // 2)).start()

    def middle(self):
        p = self.p
        drain(self.team_buf.at[pl.ds(0, 7)], self.sems.at[1])
        ref = self.plane_buf.at[p.z * 4 + p.x]
        ref[...] = jnp.sum(self.team_buf[...], 0)

        @pl.loop(1, 16)
        def _(k):
            dev = p.plane((p.x + k % 4) % 4, (p.z + k // 4) % 4)
            remote(ref, ref, self.sems.at[2], self.sems.at[3], dev).start()

        drain(self.team_buf.at[pl.ds(0, 7)], self.sems.at[0])

    def end(self):
        drain(self.plane_buf.at[pl.ds(0, 15)], self.sems.at[3])
        total = jnp.sum(self.plane_buf[...], 0)
        drain(self.plane_buf.at[pl.ds(0, 15)], self.sems.at[2])
        return total


class Swap:
    def __init__(self, place, src, dst, sems, there=None):
        self.p, self.src, self.dst, self.sems = place, src, dst, sems
        self.there = dst if there is None else there

    def far(self):
        return remote(self.src, self.there, self.sems.at[0], self.sems.at[1], self.p.partner())

    def near(self):
        return pltpu.make_async_copy(self.src, self.dst, self.sems.at[2])

    def start(self):
        self.start_far()
        self.start_near()

    def start_far(self):
        pl.when(self.p.mover)(lambda: self.far().start())

    def start_near(self):
        pl.when(jnp.logical_not(self.p.mover))(lambda: self.near().start())

    def wait(self):
        pl.when(self.p.mover)(lambda: self.far().wait())
        pl.when(jnp.logical_not(self.p.mover))(lambda: self.near().wait())


class Fetch:
    def __init__(self, place, src, dst, part, sems):
        self.p, self.src, self.dst, self.part, self.sems = place, src, dst, part, sems

    def far(self, role):
        p = self.p
        step = 1 + 2 * ((p.x + role) % 2)
        part = self.part(role)
        return remote(
            self.src.at[part],
            self.dst.at[part],
            self.sems.at[role],
            self.sems.at[2 + role],
            p.plane((p.x + step) % 4, p.z, p.xlo),
        )

    def near(self):
        return pltpu.make_async_copy(self.src, self.dst, self.sems.at[4])

    def start(self):
        self.start_away()
        self.start_partner()

    def start_away(self):
        pl.when(self.p.mover)(lambda: self.far(1).start())
        pl.when(jnp.logical_not(self.p.mover))(lambda: self.near().start())

    def start_partner(self):
        pl.when(self.p.mover)(lambda: self.far(0).start())

    def wait(self):
        @pl.when(self.p.mover)
        def _():
            self.far(0).wait()
            self.far(1).wait()

        pl.when(jnp.logical_not(self.p.mover))(lambda: self.near().wait())


class WholeWeight:
    def __init__(self, place, src, buf, sems):
        self.p, self.src, self.buf, self.sems = place, src, buf, sems

    def near(self):
        p = self.p
        return pltpu.make_async_copy(
            self.src, self.buf.at[rows((2 * p.y + p.xlo) * B, B)], self.sems.at[18]
        )

    def msg(self, i):
        p = self.p
        right, left = p.team(p.c, p.right), p.team(p.c, p.left)
        sib = p.team(1 - p.c, p.y)
        side = p.plane((p.x + 1 + 2 * p.c) % 4, p.z)
        ys = (p.y, p.left, p.right, p.opp)
        first, size = 0, 64
        if i < 6:
            y, first, size, dev = (
                (p.y, 0, 32, right),
                (p.y, 32, 32, left),
                (p.y, 32, 32, right),
                (p.y, 0, 32, left),
                (p.left, 0, 32, right),
                (p.right, 32, 32, left),
            )[i]
            group = p.xlo
        elif i < 10:
            y, group, dev = ys[i - 6], p.xlo, side
        elif i < 13:
            y, group, dev = ys[i - 9], p.xlo, sib
        else:
            y, group, dev = ys[i - 13], 1 - p.xlo, sib
        ref = self.buf.at[rows((2 * y + group) * B + p.c * 64 + first, size)]
        return remote(ref, ref, self.sems.at[17], self.sems.at[i], dev)

    def go(self, *which):
        for i in which:
            self.msg(i).start()

    def got(self, *which):
        for i in which:
            self.msg(i).wait_recv()

    def w0(self):
        self.near().wait()
        self.go(0, 1, 2, 3)

    def w1(self):
        self.go(6)
        self.got(0)
        self.go(4)
        self.got(1)
        self.go(5)
        self.got(2)
        self.go(7, 10)
        self.got(3)
        self.go(8, 11)

    def w2(self):
        self.got(4, 5)
        self.go(9, 12)

    def w3(self):
        for i in range(4):
            self.got(6 + i)
            self.go(13 + i)

    def w4(self):
        self.got(*range(10, 17))
        drain(self.buf.at[pl.ds(0, 896)], self.sems.at[17])


class Ring:
    def __init__(self, i, right, left, blk, bufs, sems):
        self.i, self.right, self.left, self.blk = i, right, left, blk
        self.bufs, self.sems = bufs, sems

    def msg(self, k):
        i, blk, bufs = self.i, self.blk, self.bufs
        src, slot, dev = (
            (lambda: blk((i + 2) % 4, 0), 0, self.right),
            (lambda: blk((i + 2) % 4, 1), 1, self.left),
            (lambda: blk((i + 1) % 4, 1), 5, self.right),
            (lambda: bufs.at[2], 4, self.right),
            (lambda: blk((i + 3) % 4, 0), 6, self.left),
            (lambda: bufs.at[3], 7, self.left),
        )[k]
        return remote(src(), bufs.at[slot], self.sems.at[6], self.sems.at[k], dev)

    def s0(self):
        for k in (0, 1, 2, 4):
            self.msg(k).start()

    def s1(self):
        bufs = self.bufs
        self.msg(0).wait_recv()
        bufs[2] = (self.blk((self.i + 1) % 4, 0)[...].astype(F32) + bufs[0].astype(F32)).astype(BF)
        self.msg(3).start()
        self.msg(1).wait_recv()
        bufs[3] = (self.blk((self.i + 3) % 4, 1)[...].astype(F32) + bufs[1].astype(F32)).astype(BF)
        self.msg(5).start()

    def s2(self, store):
        bufs = self.bufs
        for k in range(2, 6):
            self.msg(k).wait_recv()
        for h in range(2):
            total = self.blk(self.i, h)[...].astype(F32)
            total = total + bufs[4 + h].astype(F32) + bufs[6 + h].astype(F32)
            store(h, total.astype(BF))

    def sent(self):
        drain(self.bufs.at[pl.ds(0, 6)], self.sems.at[6])


class PlaneSum:
    def __init__(self, place, full, big, res, small, mine, out, sems, back, spare):
        p = self.p = place
        self.full, self.mine, self.out, self.back, self.res = full, mine, out, back, res
        self.sends = spare
        half = pl.ds(0, 512), pl.ds(512, 512)
        along_z = p.z, p.plane(p.x, (p.z + 1) % 4), p.plane(p.x, (p.z + 3) % 4)
        along_x = p.x, p.plane((p.x + 1) % 4, p.z), p.plane((p.x + 3) % 4, p.z)
        self.first = (
            Ring(
                *along_z, lambda j, h: full.at[j, pl.ds(2 * h, 2), :, half[0]],
                big.at[0], sems.at[0],
            ),
            Ring(
                *along_x, lambda j, h: full.at[pl.ds(2 * h, 2), j, :, half[1]],
                big.at[1], sems.at[1],
            ),
        )
        self.second = tuple(
            Ring(
                *along, lambda j, h, n=n: res.at[n, j, :, pl.ds(h * 256, 256)],
                small.at[n], sems.at[2 + n],
            )
            for n, along in enumerate((along_x, along_z))
        )

    def to_second(self):
        for n in range(2):

            def store(h, value, n=n):
                self.res[n, 2 * h : 2 * h + 2] = value

            self.first[n].s2(store)
            self.second[n].s0()

    def to_mine(self):
        for n in range(2):

            def store(h, value, n=n):
                self.mine[:, n * 512 + h * 256 : n * 512 + h * 256 + 256] = value

            self.second[n].s2(store)

    def side(self, i):
        p = self.p
        return remote(
            self.mine,
            self.out.at[p.z, p.x],
            self.back.at[15],
            self.back.at[11 + i],
            p.plane((p.x + (1, 3, 2)[i]) % 4, p.z),
        )

    def msg(self, i):
        p = self.p
        lt, rt, op = (p.z + 3) % 4, (p.z + 1) % 4, (p.z + 2) % 4
        right, left, sib = p.plane(p.x, rt), p.plane(p.x, lt), p.team(1 - p.c, p.y)
        block, first, size, dev = (
            (p.z, 0, 2, right),
            (p.z, 2, 2, left),
            (p.z, 2, 2, right),
            (p.z, 0, 2, left),
            (p.z, 0, 4, sib),
            (lt, 0, 2, right),
            (rt, 2, 2, left),
            (lt, 0, 4, sib),
            (rt, 0, 4, sib),
            (op, 0, 2, sib),
            (op, 2, 2, sib),
        )[i]
        ref = self.out.at[block, pl.ds(first, size)]
        return remote(ref, ref, self.back.at[14], self.back.at[i], dev)

    def g0(self):
        p = self.p

        @pl.when(p.mover)
        def _():
            self.side(0).start()
            self.side(1).start()

        @pl.when(jnp.logical_not(p.mover))
        def _():
            self.side(2).start()
            self.out[p.z, p.x] = self.mine[...]

    def stays(self, body):
        pl.when(jnp.logical_not(self.p.mover))(body)

    def g1(self):
        @self.stays
        def _():
            for i in range(3):
                self.side(i).wait_recv()
            for i in range(5):
                self.msg(i).start()

    def g2(self):
        @self.stays
        def _():
            for i in range(4):
                self.msg(i).wait_recv()
                self.msg((5, 6, 7, 8)[i]).start()

    def g3(self):
        @self.stays
        def _():
            for i in (5, 6):
                self.msg(i).wait_recv()
                self.msg(4 + i).start()

    def finish(self):
        @pl.when(self.p.mover)
        def _():
            for i in (4, 7, 8, 9, 10):
                self.msg(i).wait_recv()
            drain(self.full.at[0, pl.ds(0, 2)], self.back.at[15])

        @self.stays
        def _():
            drain(self.mine, self.back.at[15])
            for _ in range(2):
                drain(self.sends.at[pl.ds(0, 896)], self.back.at[14])

        for ring in self.first + self.second:
            ring.sent()


class Exchange:
    def __init__(self, place, src_of, dst, everything, sems):
        self.p, self.src_of, self.dst, self.all, self.sems = place, src_of, dst, everything, sems

    def msg(self, k):
        p = self.p
        j = (p.me + k) % 8
        return remote(
            self.src_of(j), self.dst, self.sems.at[0], self.sems.at[k], p.team(j % 2, j // 2)
        )

    def start_pair(self, yy):
        for core in range(2):
            k = (2 * yy + core + 8 - self.p.me) % 8
            pl.when(k != 0)(lambda: self.msg(k).start())

    def wait_pair(self, yy):
        for core in range(2):
            k = (self.p.me + 8 - (2 * yy + core)) % 8
            pl.when(k != 0)(lambda: self.msg(k).wait_recv())

    def start(self):
        @pl.loop(1, 8)
        def _(k):
            self.msg(k).start()

    def wait(self):
        @pl.loop(1, 8)
        def _(k):
            self.msg(k).wait_recv()

    def sent(self):
        drain(self.all.at[pl.ds(0, 896)], self.sems.at[0])


SCRATCH = dict(
    tok=((B, D), BF),
    gain1=((1, D), F32),
    gain2=((1, D), F32),
    cosine=((T, B), F32),
    signed=((T, B), F32),
    h1here=((B, D), BF),
    xb=((B, D), BF),
    cotb=((T, D), BF),
    w=((384, D), BF),
    wo=((T, D), BF),
    wg=((2, FF, D), BF),
    wm=((FF, D), BF),
    h1=((T, D), BF),
    h2=((T, D), BF),
    gb=((T, D), BF),
    y1=((B, D), F32),
    xhat2=((B, D), F32),
    inv2=((B, 1), F32),
    gy=((B, D), F32),
    q=((T, B), BF),
    qt=((2, B, T), BF),
    k=((T, B), BF),
    kt=((B, T), BF),
    v=((T, B), BF),
    vt=((2, 80, T), BF),
    pt=((2, T, T), BF),
    linv=((2, 1, T), F32),
    ot=((B, T), F32),
    o=((T, B), BF),
    orow=((B, D), BF),
    dorow=((B, D), BF),
    dob=((T, B), BF),
    dos=((T, B), BF),
    ds=((2, T, T), BF),
    dqt=((B, T), F32),
    dqkvt=((384, T), BF),
    m=((T, FF), BF),
    da=((T, FF), BF),
    db=((T, FF), BF),
    mt=((FR, T), BF),
    dat=((FR, T), BF),
    dbt=((FR, T), BF),
    gm=((4, 4, 64, D), BF),
    gm_big=((2, 8, 2, 64, 512), BF),
    gm_res=((2, 4, 64, 512), BF),
    gm_small=((2, 8, 64, 256), BF),
    gm_mine=((64, D), BF),
    gm_out=((4, 4, 64, D), BF),
    ga=((512, D), BF),
    ga_slots=((16, 256, B), BF),
    ga_mine=((256, B), BF),
    ga_out=((512, D), BF),
    g1t=((8, 1, D), F32),
    g1p=((16, 1, D), F32),
    g2t=((8, 1, D), F32),
    g2p=((16, 1, D), F32),
    lo_here=((B, D), BF),
    lo_out=((B, D), BF),
    tg_here=((B, D), BF),
    tg_out=((B, D), BF),
)
for _name in ("r2", "ro", "r1"):
    SCRATCH.update(
        {
            _name + "_got": ((512, D), BF),
            _name + "_held": ((512, D), BF),
            _name + "_top": ((64, D), BF),
            _name + "_bottom": ((64, D), BF),
            _name + "_left": ((B, D), BF),
            _name + "_right": ((B, D), BF),
        }
    )
SCRATCH["r2_part"] = ((T, D), BF)
SEMS = dict(
    ag_h1=(12,), ag_wo=(19,), ag_cot=(12,), ag_h2=(12,), ag_gb=(12,),
    rs_r2=(11,), rs_ro=(11,), rs_r1=(11,),
    sm=(4, 7), sm_back=(16,), sa=(12,), g1=(4,), g2=(4,),
    sw_h=(4,), sw_x=(3,), sw_cot=(3,), sw_lo=(3,), sw_tg=(3,),
    f_w=(5,), f_wg=(5,), f_wm=(5,), x_o=(8,), x_do=(8,), outs=(4,), loads=(5,),
)


def kernel(
    tok_in, cot, win, wout, wgate, wmix, gain1_in, gain2_in, cosine_in, signed_in,
    lo_ref, tg_ref, ga_ref, gm_ref, gains_ref, *scratch
):
    names = list(SCRATCH) + ["s_" + n for n in SEMS]
    s = dict(zip(names, scratch, strict=True))
    p = Place()

    class R:
        pass

    r = R()
    r.__dict__.update(s)
    tok, gain1, gain2, cosine, signed = r.tok, r.gain1, r.gain2, r.cosine, r.signed
    loads = [
        pltpu.make_async_copy(src, dst, r.s_loads.at[i])
        for i, (src, dst) in enumerate(
            ((tok_in, tok), (gain1_in, gain1), (cosine_in, cosine), (signed_in, signed), (gain2_in, gain2))
        )
    ]
    loads[0].start()
    loads[1].start()
    own = rows(p.me * B, B)
    other = rows((2 * p.y + 1 - p.c) * B, B)
    own_cols = cols(p.me * B, B)

    def gather(buf, name):
        return Gather(p, buf, s["s_ag_" + name])

    def scatter(name):
        part = r.h2 if name == "r1" else r.r2_part
        parts = [s[name + "_" + n] for n in ("got", "held", "top", "bottom", "left", "right")]
        return Scatter(p, part, *parts, s["s_rs_" + name])

    barrier = pltpu.get_barrier_semaphore()

    @pl.loop(1, 8)
    def _(k):
        j = (p.me + k) % 8
        pl.semaphore_signal(barrier, inc=1, device_id=p.team(j % 2, j // 2), device_id_type=MESH)

    @pl.loop(1, 16)
    def _(k):
        dev = p.plane((p.x + k % 4) % 4, (p.z + k // 4) % 4)
        pl.semaphore_signal(barrier, inc=1, device_id=dev, device_id_type=MESH)

    for d in (1, 3):
        dev = p.plane((p.x + d) % 4, p.z, 1 - p.c)
        pl.semaphore_signal(barrier, inc=1, device_id=dev, device_id_type=MESH)

    for load in loads[2:]:
        load.start()
    loads[0].wait()
    loads[1].wait()
    xhat, _ = norm(tok[...].astype(F32))
    h1here = (xhat * gain1[...]).astype(BF)
    r.h1here[...] = h1here
    pl.when(jnp.logical_not(p.mover))(lambda: r.h1.__setitem__((own, slice(None)), h1here))
    r.qt[...] = jnp.zeros_like(r.qt)
    r.vt[:, 64:80, :] = jnp.ones((2, 16, T), BF)
    r.mt[FF:FR, :] = jnp.zeros((FR - FF, T), BF)
    r.dat[FF:FR, :] = jnp.zeros((FR - FF, T), BF)
    r.dbt[FF:FR, :] = jnp.zeros((FR - FF, T), BF)
    whole_wo = WholeWeight(p, wout, r.wo, r.s_ag_wo)
    whole_wo.near().start()
    sw_cot = Swap(p, cot, r.cotb.at[own], r.s_sw_cot, r.cotb.at[other])
    sw_cot.start_near()
    pl.semaphore_wait(barrier, 24)

    def sw_h(i):
        return remote(
            r.h1here.at[rows(i * 64, 64)],
            r.h1.at[rows((2 * p.y + 1 - p.c) * B + i * 64, 64)],
            r.s_sw_h.at[i],
            r.s_sw_h.at[2 + i],
            p.partner(),
        )

    f_w = Fetch(p, win, r.w, lambda role: rows(role * 128, 128 + role * 128), r.s_f_w)
    f_wg = Fetch(p, wgate, r.wg, lambda i: (slice(None), slice(None), cols(i * 512, 512)), r.s_f_wg)
    f_wm = Fetch(p, wmix, r.wm, lambda i: (slice(None), cols(i * 512, 512)), r.s_f_wm)
    sw_x = Swap(p, tok, r.xb, r.s_sw_x)
    ag_h1, ag_h2, ag_gb = gather(r.h1, "h1"), gather(r.h2, "h2"), gather(r.gb, "gb")
    ag_cot = gather(r.cotb, "cot")

    @pl.when(p.mover)
    def _():
        sw_h(0).start()
        sw_h(1).start()

    f_w.start()
    pl.when(jnp.logical_not(p.mover))(lambda: ag_h1.start())
    whole_wo.w0()
    sw_cot.start_far()

    @pl.when(p.mover)
    def _():
        sw_h(0).wait()
        ag_h1.start_top()
        sw_h(1).wait()
        ag_h1.start_bottom()

    ag_h1.second()
    whole_wo.w1()
    sw_x.start()
    f_w.wait()
    for load in loads[2:]:
        load.wait()

    def project(yy):
        at = rows(yy * 256, 256)
        lanes = cols(yy * 256, 256)
        u = nt(r.h1[at, :], r.w[...])
        co, si = cosine[at, :], signed[at, :]
        q = u[:, :128]
        q = (q * co + swap_halves(q) * si) * (0.125 * LOG2E)
        r.q[at, :] = q.astype(BF)
        qt = q.T.astype(BF)
        r.qt[0, 0:64, lanes] = qt[0:64]
        r.qt[1, 64:128, lanes] = qt[64:128]
        k = u[:, 128:256]
        k = k * co + swap_halves(k) * si
        r.k[at, :] = k.astype(BF)
        r.kt[:, lanes] = k.T.astype(BF)
        v = u[:, 256:]
        r.v[at, :] = v.astype(BF)
        vt = v.T.astype(BF)
        r.vt[0, 0:64, lanes] = vt[0:64]
        r.vt[1, 0:64, lanes] = vt[64:128]

    def early(step):
        @pl.when(step == 3)
        def _():
            sw_cot.wait()
            ag_cot.start()
            whole_wo.w2()
            f_wg.start()
            f_wm.start()

    ag_h1.steps(project, early, True)

    x_o = Exchange(
        p, lambda j: r.o.at[rows(j * B, B)], r.orow.at[:, own_cols], r.o, r.s_x_o
    )

    @pl.loop(0, 4)
    def _(step):
        yy = (p.y + pick(step, 2, 1, 3, 0)) % 4
        lanes = cols(yy * 256, 256)

        pl.when(step == 3)(whole_wo.w3)
        scores = [nn(r.k[...], r.qt[h, :, lanes]) for h in range(2)]
        parts = []
        for h in range(2):
            probs = jnp.exp2(scores[h] - jnp.max(scores[h], 0, keepdims=True)).astype(BF)
            r.pt[h, :, lanes] = probs
            acc = nn(r.vt[h], probs)
            inverse = 1.0 / acc[64:65]
            r.linv[h, :, lanes] = inverse
            parts.append(acc[0:64] * inverse)
        ot = jnp.concatenate(parts, 0)
        r.ot[:, lanes] = ot
        r.o[rows(yy * 256, 256), :] = ot.T.astype(BF)
        x_o.start_pair(yy)

    r.orow[:, own_cols] = r.o[own, :]
    ag_cot.first()
    ag_cot.second()
    sw_x.wait()
    whole_wo.w4()
    x_o.wait()

    x = r.xb[...].astype(F32)
    y1 = x + nn(r.orow[...], r.wo[...])
    r.y1[...] = y1
    xhat, inverse = norm(y1)
    r.xhat2[...] = xhat
    r.inv2[...] = inverse
    r.h2[own, :] = (xhat * gain2[...]).astype(BF)
    ag_h2.start()
    x_o.sent()
    ag_cot.third()
    f_wg.wait()
    f_wm.wait()
    ag_cot.rest()

    def mix(yy):
        at = rows(yy * 256, 256)
        lanes = cols(yy * 256, 256)
        h2 = r.h2[at, :]
        a = nt(h2, r.wg[0])
        b = nt(h2, r.wg[1])
        cdf = 0.5 * (1.0 + lax.erf(a * 0.7071067811865476))
        gelu = a * cdf
        slope = cdf + a * (jnp.exp(-0.5 * a * a) * 0.3989422804014327)
        m = gelu * b
        dm = nt(r.cotb[at, :], r.wm[...]).astype(BF).astype(F32)
        da = dm * b * slope
        db = dm * gelu
        r.m[at, :] = m.astype(BF)
        r.da[at, :] = da.astype(BF)
        r.db[at, :] = db.astype(BF)
        r.mt[0:FF, lanes] = m.T.astype(BF)
        r.dat[0:FF, lanes] = da.T.astype(BF)
        r.dbt[0:FF, lanes] = db.T.astype(BF)

    ag_h2.steps(mix)

    def back_mix(yy):
        at = rows(yy * 256, 256)
        return nn(r.da[at, :], r.wg[0]) + nn(r.db[at, :], r.wg[1])

    rs_2 = scatter("r2")
    rs_2.phase(back_mix)
    sums_m = PlaneSum(
        p, r.gm, r.gm_big, r.gm_res, r.gm_small, r.gm_mine, r.gm_out, r.s_sm, r.s_sm_back, r.r2_part
    )

    def mix_grads(i):
        lanes = cols(i * 256, 256)
        grads = [
            nn(r.mt[...], r.cotb[:, lanes]).astype(BF),
            nn(r.dat[...], r.h2[:, lanes]).astype(BF),
            nn(r.dbt[...], r.h2[:, lanes]).astype(BF),
            jnp.zeros((1024 - 3 * FR, 256), BF),
        ]
        r.gm[:, :, :, lanes] = jnp.concatenate(grads, 0).reshape(4, 4, 64, 256)

    pl.loop(0, 2)(mix_grads)
    sums_m.first[0].s0()
    rs_2.step1()
    pl.loop(2, 4)(mix_grads)
    sums_m.first[1].s0()
    dh2 = rs_2.step2()
    sums_m.first[0].s1()
    sums_m.first[1].s1()

    dx, dgain2 = norm_back(dh2, r.xhat2[...], r.inv2[...], gain2[...])
    gy = r.cotb[own, :].astype(F32) + dx
    r.gy[...] = gy
    r.gb[own, :] = gy.astype(BF)
    r.dorow[...] = nt(r.gb[own, :], r.wo[...]).astype(BF)
    x_do = Exchange(
        p, lambda j: r.dorow.at[:, cols(j * B, B)], r.dob.at[own], r.dob, r.s_x_do
    )
    x_do.start()
    r.dob[own, :] = r.dorow[:, own_cols]
    ag_gb.start()
    gain_2 = Gain(p, r.g2t, r.g2p, r.s_g2)
    gain_2.start(dgain2)
    rs_o = scatter("ro")
    rs_o.phase(lambda yy: nn(r.m[rows(yy * 256, 256), :], r.wm[...]), False)

    @pl.loop(0, 4)
    def _(step):
        yy = (p.y + pick(step, 0, 3, 1, 2)) % 4
        at = rows(yy * 256, 256)
        lanes = cols(yy * 256, 256)

        pl.when(step == 1)(sums_m.to_second)

        @pl.when(step == 3)
        def _():
            sums_m.second[0].s1()
            sums_m.second[1].s1()

        x_do.wait_pair(yy)
        dot = r.dob[at, :].astype(F32).T
        zero = jnp.zeros((64, 256), BF)
        scaled = []
        for h in range(2):
            half = dot[h * 64 : h * 64 + 64] * r.linv[h, :, lanes]
            scaled.append(half)
        dpt = [
            nn(r.v[...], jnp.concatenate([scaled[0].astype(BF), zero], 0)),
            nn(r.v[...], jnp.concatenate([zero, scaled[1].astype(BF)], 0)),
        ]
        r.dos[at, :] = jnp.concatenate(scaled, 0).T.astype(BF)
        for h in range(2):
            half = slice(h * 64, h * 64 + 64)
            weighted = jnp.sum(scaled[h] * r.ot[half, lanes], 0, keepdims=True)
            ds = (r.pt[h, :, lanes].astype(F32) * (dpt[h] - weighted)).astype(BF)
            r.ds[h, :, lanes] = ds
            r.dqt[half, lanes] = nn(r.kt[half, :], ds)

    x_do.sent()

    def back_project(yy):
        at = rows(yy * 256, 256)
        lanes = cols(yy * 256, 256)
        first = lax.broadcasted_iota(jnp.int32, (256, B), 1) < 64
        dk = jnp.where(first, nn(r.ds[0, at, :], r.q[...]), nn(r.ds[1, at, :], r.q[...])) * (1 / LOG2E)
        dv = jnp.where(first, nn(r.pt[0, at, :], r.dos[...]), nn(r.pt[1, at, :], r.dos[...]))
        co, si = cosine[at, :], signed[at, :]
        dq = r.dqt[:, lanes].T * 0.125
        dq = dq * co - swap_halves(dq) * si
        dk = dk * co - swap_halves(dk) * si
        r.dqkvt[0:128, lanes] = dq.T.astype(BF)
        r.dqkvt[128:256, lanes] = dk.T.astype(BF)
        r.dqkvt[256:384, lanes] = dv.T.astype(BF)
        dqkv = jnp.concatenate([dq.astype(BF), dk.astype(BF), dv.astype(BF)], 1)
        return nn(dqkv, r.w[...])

    rs_1 = scatter("r1")

    def late(step):
        @pl.when(step == 0)
        def _():
            ag_gb.first()
            ag_gb.second()

        @pl.when(step == 1)
        def _():
            sums_m.to_mine()
            sums_m.g0()

    rs_1.phase(back_project, True, late)
    rs_1.step1()
    sums_m.g1()
    sums_a = Sums(
        p, r.ga, r.ga_slots, r.ga_mine, r.ga_out, r.s_sa
    )
    ag_gb.third()
    ag_gb.rest()

    @pl.loop(0, 4)
    def _(i):
        off = (i + 2) % 4
        lanes = cols(((p.z + off) % 4) * 256, 256)
        r.ga[0:384, lanes] = nn(r.dqkvt[...], r.h1[:, lanes]).astype(BF)
        r.ga[384:512, lanes] = nn(r.ot[...].astype(BF), r.gb[:, lanes]).astype(BF)
        sums_a.spread(off)

    rs_o.step0()
    rs_o.step_right()
    rs_o.step_left()
    dh1 = rs_1.step2()
    xhat, inverse = norm(r.xb[...].astype(F32))
    dx, dgain1 = norm_back(dh1, xhat, inverse, gain1[...])
    gain_1 = Gain(p, r.g1t, r.g1p, r.s_g1)
    gain_1.start(dgain1)
    r.tg_here[...] = (r.gy[...] + dx).astype(BF)
    sw_tg = Swap(p, r.tg_here, r.tg_out, r.s_sw_tg)
    sw_tg.start()
    sums_m.g2()
    rs_o.step1()
    sums_a.add()
    sums_a.give()
    gain_2.middle()
    gain_1.middle()
    r.lo_here[...] = (r.y1[...] + rs_o.step2()).astype(BF)
    sw_lo = Swap(p, r.lo_here, r.lo_out, r.s_sw_lo)
    sw_lo.start()
    sw_tg.wait()
    tg_copy = pltpu.make_async_copy(r.tg_out, tg_ref, r.s_outs.at[0])
    tg_copy.start()
    sums_m.g3()
    sums_a.take()
    sums_m.finish()
    gm_copy = pltpu.make_async_copy(r.gm_out, gm_ref, r.s_outs.at[1])
    gm_copy.start()
    gains_ref[1:2, :] = gain_2.end()
    gains_ref[0:1, :] = gain_1.end()
    sw_lo.wait()
    lo_copy = pltpu.make_async_copy(r.lo_out, lo_ref, r.s_outs.at[2])
    lo_copy.start()
    sums_a.finish()
    ga_copy = pltpu.make_async_copy(r.ga_out, ga_ref, r.s_outs.at[3])
    ga_copy.start()
    for copy in [lo_copy, tg_copy, gm_copy, ga_copy]:
        copy.wait()


def widen(
    lo, tg, ga, gm, gains, lo_ref, tg_ref, gi_ref, go_ref, gg_ref, gm_ref, first_ref, second_ref,
    lo_in, tg_in, ga_in, gm_in, tg_out, ga_out, gm_out, sems,
):
    pieces = [(gm, gm_in, gm_out, i * FR, FF, target) for i, target in enumerate((gm_ref, gg_ref.at[0], gg_ref.at[1]))]
    pieces += [(ga, ga_in, ga_out, 0, 384, gi_ref), (ga, ga_in, ga_out, 384, B, go_ref)]
    pieces += [(tg, tg_in, tg_out, 0, B, tg_ref)]
    loads, stores = [], []
    for i, (src, held, _, first, size, _) in enumerate(pieces):
        part = pl.ds(first, FR if size == FF else size)
        loads.append(pltpu.make_async_copy(src.at[part], held.at[part], sems.at[i]))
    loads.append(pltpu.make_async_copy(lo, lo_in, sems.at[6]))
    for load in loads:
        load.start()
    for i in range(8):
        first_ref[i : i + 1, :] = gains[0:1, i * B : i * B + B]
        second_ref[i : i + 1, :] = gains[1:2, i * B : i * B + B]
    for i, (_, held, wide, first, size, target) in enumerate(pieces):
        loads[i].wait()
        wide[first : first + size, :] = held[first : first + size, :].astype(F32)
        stores.append(pltpu.make_async_copy(wide.at[pl.ds(first, size)], target, sems.at[7 + i]))
        stores[-1].start()
    loads[6].wait()
    stores.append(pltpu.make_async_copy(lo_in, lo_ref, sems.at[13]))
    stores[-1].start()
    for store in stores:
        store.wait()


def local(tokens, attn_in, attn_out, mlp_in, mlp_out, norm_first, norm_second, cotangent):
    cosine, signed = tables()
    any_space = pl.BlockSpec(memory_space=pl.ANY)
    vmem = pl.BlockSpec(memory_space=pltpu.VMEM)
    limit = 63 * 1024 * 1024
    shapes = [(B, D), (B, D), (512, D), (4, 4, 64, D)]
    lo, tg, ga, gm, gains = pl.pallas_call(
        kernel,
        out_shape=tuple(jax.ShapeDtypeStruct(shape, BF) for shape in shapes)
        + (jax.ShapeDtypeStruct((2, D), F32),),
        in_specs=[any_space] * 10,
        out_specs=(any_space,) * 4 + (vmem,),
        scratch_shapes=[pltpu.VMEM(shape, kind) for shape, kind in SCRATCH.values()]
        + [pltpu.SemaphoreType.DMA(shape) for shape in SEMS.values()],
        compiler_params=pltpu.CompilerParams(
            collective_id=0, has_side_effects=True, vmem_limit_bytes=limit
        ),
    )(
        tokens,
        cotangent,
        attn_in.transpose(1, 2, 3, 0).reshape(384, D),
        attn_out.reshape(B, D),
        mlp_in.transpose(0, 2, 1),
        mlp_out,
        norm_first.reshape(1, D),
        norm_second.reshape(1, D),
        jnp.asarray(cosine),
        jnp.asarray(signed),
    )
    wide = [(B, D), (384, D), (B, D), (2, FF, D), (FF, D), (8, B), (8, B)]
    lo, tg, gi, go, gg, gm, first, second = pl.pallas_call(
        widen,
        out_shape=(jax.ShapeDtypeStruct((B, D), BF),)
        + tuple(jax.ShapeDtypeStruct(shape, F32) for shape in wide),
        in_specs=[any_space] * 4 + [vmem],
        out_specs=(any_space,) * 6 + (vmem, vmem),
        scratch_shapes=[
            pltpu.VMEM((B, D), BF),
            pltpu.VMEM((B, D), BF),
            pltpu.VMEM((512, D), BF),
            pltpu.VMEM((1024, D), BF),
            pltpu.VMEM((B, D), F32),
            pltpu.VMEM((512, D), F32),
            pltpu.VMEM((3 * FR, D), F32),
            pltpu.SemaphoreType.DMA((14,)),
        ],
        compiler_params=pltpu.CompilerParams(vmem_limit_bytes=limit),
    )(lo, tg, ga, gm.reshape(1024, D), gains)
    return (
        lo,
        tg,
        gi.reshape(3, 2, 64, D).transpose(3, 0, 1, 2),
        go.reshape(2, 64, D),
        gg.transpose(0, 2, 1),
        gm,
        first.reshape(D),
        second.reshape(D),
    )


def solution(mesh):
    placed = (
        P(("dp", "tensor"), None),
        P(None, None, "tensor", None),
        P("tensor", None, None),
        P(None, None, "tensor"),
        P("tensor", None),
        P(),
        P(),
        P(("dp", "tensor"), None),
    )
    return jax.shard_map(
        local,
        mesh=mesh,
        in_specs=placed,
        out_specs=(
            P(("dp", "tensor"), None),
            P(("dp", "tensor"), None),
            P(None, None, "tensor", None),
            P("tensor", None, None),
            P(None, None, "tensor"),
            P("tensor", None),
            P(),
            P(),
        ),
        check_vma=False,
    )
```

time: 178 us -> 126 us (0.71)
  Pallas kernels: 163 us -> 125 us
  other arithmetic: 7.53 us -> 0 us
  local copies, waits for them, and re-layouts: 6.62 us -> 0 us
    pallas_call x1 -> x2, Pallas kernels: 163 us -> 125 us  [the longest x1 120 us: local(): pl.pallas_call(kernel, out_shape=tuple((jax.ShapeDtypeStruct(shape, BF) f...]
    convert_element_type x2 -> x0, other arithmetic: 3.68 us -> none  [the longest x1 2.84 us: local(): mlp_out_grad = gm[:FF].astype(F32)]
    unnamed x14 -> x0, local copies, waits for them, and re-layouts: 2.56 us -> none
    pad x2 -> x0, local copies, waits for them, and re-layouts: 2.28 us -> none  [the longest x1 1.32 us: local(): jnp.pad(mlp_in, ((0, 0), (0, 0), (0, FP - FF)))]
    reshape x2 -> x0, other arithmetic: 2.16 us -> none  [the longest x1 1.32 us: local(): attn_in_grad = ga[:384].astype(F32).T.reshape(D, 3, 2, 64)]
where the time goes in v2:
time: 126 us
  Pallas kernels  125 us (99%)
    pallas_call x1, Pallas kernels, local(): pl.pallas_call(kernel, out_shape=tuple((jax.ShapeDtypeStruct(shape, BF) f...  120 us
    pallas_call x1, Pallas kernels, local(): pl.pallas_call(widen, out_shape=(jax.ShapeDtypeStruct((B, D), BF),) + tup...  5.47 us

profile of v2, /device:TPU:1, one launch (start us, length us, event | category | flops | bytes accessed | tf_op | source)
XLA Modules:
  0.0 126.1 jit_solution(11336901871908623676)
XLA Ops:
  0.6 120.0 %shard_map.161 = (bf16[128,1024]{1,0:T(8,128)(2,1)}, bf16[128,1024]{1,0:T(8,128)(2,1)}, bf16[512,1024]{1,0:T(8,128)(2,1)}, bf16[4,4,64,1024]{3,2,1,0:T(8,128)(2,1)}, f32[2,1024]{1,0:T(2,128)}) custom-call(bf16[128,1024]{1,0:T(8,128)(2,1)} %tok_in.1, bf16[128,1024]{1,0:T(8,128)(2,1)} %cot.1, bf16[384,1024]{1,0:T(8,128)(2,1)} %bitcast.17, ...), custom_call_target="tpu_custom_call" | custom-call | tf_op jit(solution)/shard_map/pallas_call | solution.py:1286
  120.6 5.5 %shard_map.162 = (bf16[128,1024]{1,0:T(8,128)(2,1)}, f32[128,1024]{1,0:T(8,128)}, f32[384,1024]{1,0:T(8,128)}, f32[128,1024]{1,0:T(8,128)}, f32[2,328,1024]{2,1,...) custom-call(bf16[128,1024]{1,0:T(8,128)(2,1)} %get-tuple-element.21.lo, ...), custom_call_target="tpu_custom_call" | custom-call | tf_op jit(solution)/shard_map/pallas_call | solution.py:1310

commit v3 on v2

--- a/solution.py
+++ b/solution.py
@@ -179,7 +179,7 @@
         self.opp_in()
         self.sent()
 
-    def steps(self, body, hook=None, forwarded=False):
+    def steps(self, body, hook=None, forwarded=False, idle=None):
         p = self.p
 
         @pl.loop(0, 4)
@@ -190,6 +190,8 @@
 
             @pl.when(step == 1)
             def _():
+                if idle is not None:
+                    idle()
                 if not forwarded:
                     self.second()
                 self.left_in()
@@ -306,112 +308,6 @@
         total = total + self.from_left[...].astype(F32) + self.from_right[...].astype(F32)
         drain(self.part.at[pl.ds(0, 896)], self.sems.at[10])
         return total
-
-
-class Sums:
-    def __init__(self, place, full, slots, mine, out, sems):
-        self.p = place
-        self.full, self.slots, self.mine, self.out = full, slots, mine, out
-        self.size = full.shape[0] // 2
-        self.sems = sems
-
-    def peer(self, k):
-        return (self.p.x + k % 4) % 4, (self.p.z + k // 4) % 4
-
-    def chunk(self, x, z):
-        return rows((x % 2) * self.size, self.size), cols((z * 2 + x // 2) * B, B)
-
-    def spread_msg(self, k):
-        x, z = self.peer(k)
-        return remote(
-            self.full.at[self.chunk(x, z)],
-            self.slots.at[k],
-            self.sems.at[0],
-            self.sems.at[1],
-            self.p.plane(x, z),
-        )
-
-    def spread(self, off):
-        @pl.loop(0, 4)
-        def _(i):
-            k = off * 4 + i
-
-            @pl.when(k != 0)
-            def _():
-                self.spread_msg(k).start()
-
-    def add(self):
-        p, size = self.p, self.size
-
-        drain(self.slots.at[pl.ds(1, 15)], self.sems.at[1])
-        own_cols = cols((p.z * 2 + p.x // 2) * B, B)
-
-        @pl.loop(0, size // 64)
-        def _(r):
-            total = self.full[rows((p.x % 2) * size + r * 64, 64), own_cols].astype(F32)
-            for k in range(1, 16):
-                total = total + self.slots[k, rows(r * 64, 64), :].astype(F32)
-            self.mine[rows(r * 64, 64), :] = total.astype(BF)
-
-    def return_msg(self, k):
-        p = self.p
-        x, z = self.peer(k)
-        return remote(
-            self.mine,
-            self.out.at[self.chunk(p.x, p.z)],
-            self.sems.at[2],
-            self.sems.at[4 + k // 4],
-            p.plane(x, z),
-        )
-
-    def goes(self, k):
-        return ((self.p.x + k % 4) % 2 == self.p.c) & (k != 0)
-
-    def give(self):
-        p = self.p
-
-        @pl.loop(0, 16)
-        def _(k):
-            @pl.when(self.goes(k))
-            def _():
-                self.return_msg(k).start()
-
-        @pl.when(jnp.logical_not(p.mover))
-        def _():
-            at, lanes = self.chunk(p.x, p.z)
-            self.out[at, lanes] = self.mine[...]
-
-    def forward(self, i):
-        p = self.p
-        block = self.out.at[:, cols(((p.z + 4 - i) % 4) * 256, 256)]
-        return remote(block, block, self.sems.at[3], self.sems.at[8 + i], p.team(1 - p.c, p.y))
-
-    def take(self):
-        p = self.p
-
-        @pl.when(jnp.logical_not(p.mover))
-        def _():
-            for i in range(4):
-                drain(self.slots.at[pl.ds(0, 4 if i else 3)], self.sems.at[4 + i])
-                self.forward(i).start()
-
-    def finish(self):
-        p = self.p
-
-        @pl.when(p.mover)
-        def _():
-            @pl.loop(0, 4)
-            def _(i):
-                self.forward(i).wait_recv()
-
-            drain(self.slots.at[pl.ds(0, 8)], self.sems.at[2])
-
-        @pl.when(jnp.logical_not(p.mover))
-        def _():
-            drain(self.out, self.sems.at[3])
-            drain(self.slots.at[pl.ds(0, 7)], self.sems.at[2])
-
-        drain(self.slots.at[pl.ds(1, 15)], self.sems.at[0])
 
 
 class Gain:
@@ -586,92 +482,113 @@
         drain(self.buf.at[pl.ds(0, 896)], self.sems.at[17])
 
 
-class Ring:
-    def __init__(self, i, right, left, blk, bufs, sems):
-        self.i, self.right, self.left, self.blk = i, right, left, blk
-        self.bufs, self.sems = bufs, sems
-
-    def msg(self, k):
-        i, blk, bufs = self.i, self.blk, self.bufs
-        src, slot, dev = (
-            (lambda: blk((i + 2) % 4, 0), 0, self.right),
-            (lambda: blk((i + 2) % 4, 1), 1, self.left),
-            (lambda: blk((i + 1) % 4, 1), 5, self.right),
-            (lambda: bufs.at[2], 4, self.right),
-            (lambda: blk((i + 3) % 4, 0), 6, self.left),
-            (lambda: bufs.at[3], 7, self.left),
-        )[k]
-        return remote(src(), bufs.at[slot], self.sems.at[6], self.sems.at[k], dev)
-
-    def s0(self):
-        for k in (0, 1, 2, 4):
-            self.msg(k).start()
-
-    def s1(self):
-        bufs = self.bufs
-        self.msg(0).wait_recv()
-        bufs[2] = (self.blk((self.i + 1) % 4, 0)[...].astype(F32) + bufs[0].astype(F32)).astype(BF)
-        self.msg(3).start()
-        self.msg(1).wait_recv()
-        bufs[3] = (self.blk((self.i + 3) % 4, 1)[...].astype(F32) + bufs[1].astype(F32)).astype(BF)
-        self.msg(5).start()
-
-    def s2(self, store):
-        bufs = self.bufs
-        for k in range(2, 6):
-            self.msg(k).wait_recv()
-        for h in range(2):
-            total = self.blk(self.i, h)[...].astype(F32)
-            total = total + bufs[4 + h].astype(F32) + bufs[6 + h].astype(F32)
-            store(h, total.astype(BF))
+class AxisSum:
+    def __init__(self, i, dev, blk, bufs, sems):
+        self.i, self.dev, self.blk, self.bufs, self.sems = i, dev, blk, bufs, sems
+
+    def start(self):
+        for k in (2, 1, 3):
+            j = (self.i + k) % 4
+            remote(
+                self.blk(j), self.bufs.at[k - 1], self.sems.at[1], self.sems.at[0], self.dev(j)
+            ).start()
+
+    def total(self):
+        drain(self.bufs, self.sems.at[0])
+        total = self.blk(self.i)[...].astype(F32)
+        for k in range(3):
+            total = total + self.bufs[k].astype(F32)
+        return total.astype(BF)
 
     def sent(self):
-        drain(self.bufs.at[pl.ds(0, 6)], self.sems.at[6])
+        drain(self.bufs, self.sems.at[1])
 
 
 class PlaneSum:
-    def __init__(self, place, full, big, res, small, mine, out, sems, back, spare):
+    def __init__(self, place, full, big, res, small, mine, out, sems, back):
         p = self.p = place
         self.full, self.mine, self.out, self.back, self.res = full, mine, out, back, res
-        self.sends = spare
-        half = pl.ds(0, 512), pl.ds(512, 512)
-        along_z = p.z, p.plane(p.x, (p.z + 1) % 4), p.plane(p.x, (p.z + 3) % 4)
-        along_x = p.x, p.plane((p.x + 1) % 4, p.z), p.plane((p.x + 3) % 4, p.z)
+        along_z = p.z, lambda j: p.plane(p.x, j)
+        along_x = p.x, lambda j: p.plane(j, p.z)
+        self.half = half = full.shape[3] // 2
         self.first = (
-            Ring(
-                *along_z, lambda j, h: full.at[j, pl.ds(2 * h, 2), :, half[0]],
-                big.at[0], sems.at[0],
-            ),
-            Ring(
-                *along_x, lambda j, h: full.at[pl.ds(2 * h, 2), j, :, half[1]],
-                big.at[1], sems.at[1],
-            ),
+            AxisSum(*along_z, lambda j: full.at[j, :, :, pl.ds(0, half)], big.at[0], sems.at[0]),
+            AxisSum(*along_x, lambda j: full.at[:, j, :, pl.ds(half, half)], big.at[1], sems.at[1]),
         )
-        self.second = tuple(
-            Ring(
-                *along, lambda j, h, n=n: res.at[n, j, :, pl.ds(h * 256, 256)],
-                small.at[n], sems.at[2 + n],
-            )
-            for n, along in enumerate((along_x, along_z))
+        self.second = (
+            AxisSum(*along_x, lambda j: res.at[0, j], small.at[0], sems.at[2]),
+            AxisSum(*along_z, lambda j: res.at[1, j], small.at[1], sems.at[3]),
         )
 
-    def to_second(self):
-        for n in range(2):
-
-            def store(h, value, n=n):
-                self.res[n, 2 * h : 2 * h + 2] = value
-
-            self.first[n].s2(store)
-            self.second[n].s0()
+    def to_second(self, *which):
+        for n in which:
+            self.res[n] = self.first[n].total()
+            self.second[n].start()
 
     def to_mine(self):
         for n in range(2):
-
-            def store(h, value, n=n):
-                self.mine[:, n * 512 + h * 256 : n * 512 + h * 256 + 256] = value
-
-            self.second[n].s2(store)
-
+            self.mine[:, n * self.half : (n + 1) * self.half] = self.second[n].total()
+
+    def give_msg(self, k):
+        p = self.p
+        dev = p.plane((p.x + k % 4) % 4, (p.z + k // 4) % 4)
+        ref = self.out.at[p.z, p.x]
+        return remote(self.mine, ref, self.back.at[0], self.back.at[2 + k // 4], dev)
+
+    def give(self):
+        p = self.p
+
+        @pl.loop(0, 8)
+        def _(i):
+            k = (i // 2) * 4 + (i % 2) * 2 + jnp.where(p.mover, 1, 0)
+            pl.when(k != 0)(lambda: self.give_msg(k).start())
+
+        @self.stays
+        def _():
+            self.out[p.z, p.x] = self.mine[...]
+
+    def forward(self, i):
+        p = self.p
+        block = self.out.at[(p.z + 4 - i) % 4]
+        return remote(block, block, self.back.at[1], self.back.at[6 + i], p.team(1 - p.c, p.y))
+
+    def to(self, i, target, sem):
+        block = (self.p.z + 4 - i) % 4
+        return pltpu.make_async_copy(self.out.at[block], target.at[block], sem)
+
+    def take(self, target, sem):
+        @self.stays
+        def _():
+            for i in range(4):
+                drain(self.out.at[0, pl.ds(0, 4 if i else 3)], self.back.at[2 + i])
+                self.forward(i).start()
+                self.to(i, target, sem).start()
+
+        @pl.when(self.p.mover)
+        def _():
+            for i in range(4):
+                self.forward(i).wait_recv()
+                self.to(i, target, sem).start()
+
+    def taken(self):
+        @pl.when(self.p.mover)
+        def _():
+            drain(self.out.at[pl.ds(0, 2)], self.back.at[0])
+
+        @self.stays
+        def _():
+            drain(self.out, self.back.at[1])
+            drain(self.full.at[0], self.back.at[0])
+            drain(self.full.at[1, pl.ds(0, 3)], self.back.at[0])
+
+        for axis in self.first + self.second:
+            axis.sent()
+
+    def stays(self, body):
+        pl.when(jnp.logical_not(self.p.mover))(body)
+
+
+class StagedPlaneSum(PlaneSum):
     def side(self, i):
         p = self.p
         return remote(
@@ -715,9 +632,6 @@
             self.side(2).start()
             self.out[p.z, p.x] = self.mine[...]
 
-    def stays(self, body):
-        pl.when(jnp.logical_not(self.p.mover))(body)
-
     def g1(self):
         @self.stays
         def _():
@@ -750,11 +664,11 @@
         @self.stays
         def _():
             drain(self.mine, self.back.at[15])
-            for _ in range(2):
-                drain(self.sends.at[pl.ds(0, 896)], self.back.at[14])
-
-        for ring in self.first + self.second:
-            ring.sent()
+            drain(self.out, self.back.at[14])
+            drain(self.out.at[pl.ds(0, 3)], self.back.at[14])
+
+        for axis in self.first + self.second:
+            axis.sent()
 
 
 class Exchange:
@@ -773,6 +687,11 @@
             k = (2 * yy + core + 8 - self.p.me) % 8
             pl.when(k != 0)(lambda: self.msg(k).start())
 
+    def wait(self):
+        @pl.loop(1, 8)
+        def _(k):
+            self.msg(k).wait_recv()
+
     def wait_pair(self, yy):
         for core in range(2):
             k = (self.p.me + 8 - (2 * yy + core)) % 8
@@ -782,11 +701,6 @@
         @pl.loop(1, 8)
         def _(k):
             self.msg(k).start()
-
-    def wait(self):
-        @pl.loop(1, 8)
-        def _(k):
-            self.msg(k).wait_recv()
 
     def sent(self):
         drain(self.all.at[pl.ds(0, 896)], self.sems.at[0])
@@ -798,7 +712,6 @@
     gain2=((1, D), F32),
     cosine=((T, B), F32),
     signed=((T, B), F32),
-    h1here=((B, D), BF),
     xb=((B, D), BF),
     cotb=((T, D), BF),
     w=((384, D), BF),
@@ -813,6 +726,7 @@
     inv2=((B, 1), F32),
     gy=((B, D), F32),
     q=((T, B), BF),
+    dqkv=((T, 384), BF),
     qt=((2, B, T), BF),
     k=((T, B), BF),
     kt=((B, T), BF),
@@ -823,8 +737,6 @@
     ot=((B, T), F32),
     o=((T, B), BF),
     orow=((B, D), BF),
-    dorow=((B, D), BF),
-    dob=((T, B), BF),
     dos=((T, B), BF),
     ds=((2, T, T), BF),
     dqt=((B, T), F32),
@@ -836,15 +748,25 @@
     dat=((FR, T), BF),
     dbt=((FR, T), BF),
     gm=((4, 4, 64, D), BF),
-    gm_big=((2, 8, 2, 64, 512), BF),
+    gm_big=((2, 3, 4, 64, 512), BF),
     gm_res=((2, 4, 64, 512), BF),
-    gm_small=((2, 8, 64, 256), BF),
+    gm_small=((2, 3, 64, 512), BF),
     gm_mine=((64, D), BF),
     gm_out=((4, 4, 64, D), BF),
-    ga=((512, D), BF),
-    ga_slots=((16, 256, B), BF),
-    ga_mine=((256, B), BF),
-    ga_out=((512, D), BF),
+    ga=((4, 4, 48, 512), BF),
+    ga_big=((2, 3, 4, 48, 256), BF),
+    ga_res=((2, 4, 48, 256), BF),
+    ga_small=((2, 3, 48, 256), BF),
+    ga_mine=((48, 512), BF),
+    ga_out=((4, 4, 48, 512), BF),
+    go=((4, 4, 16, 512), BF),
+    go_big=((2, 3, 4, 16, 256), BF),
+    go_res=((2, 4, 16, 256), BF),
+    go_small=((2, 3, 16, 256), BF),
+    go_mine=((16, 512), BF),
+    go_out=((4, 4, 16, 512), BF),
+    dorow=((B, D), BF),
+    dob=((T, B), BF),
     g1t=((8, 1, D), F32),
     g1p=((16, 1, D), F32),
     g2t=((8, 1, D), F32),
@@ -869,15 +791,15 @@
 SEMS = dict(
     ag_h1=(12,), ag_wo=(19,), ag_cot=(12,), ag_h2=(12,), ag_gb=(12,),
     rs_r2=(11,), rs_ro=(11,), rs_r1=(11,),
-    sm=(4, 7), sm_back=(16,), sa=(12,), g1=(4,), g2=(4,),
-    sw_h=(4,), sw_x=(3,), sw_cot=(3,), sw_lo=(3,), sw_tg=(3,),
-    f_w=(5,), f_wg=(5,), f_wm=(5,), x_o=(8,), x_do=(8,), outs=(4,), loads=(5,),
+    sm=(4, 2), sm_back=(16,), sa=(4, 2), sa_back=(10,), so=(4, 2), so_back=(10,), g1=(4,), g2=(4,),
+    sw_x=(4,), sw_cot=(3,), sw_lo=(3,), sw_tg=(3,),
+    f_w=(5,), f_wg=(2, 5), f_wm=(5,), x_o=(8,), x_do=(8,), outs=(5,), loads=(5,),
 )
 
 
 def kernel(
     tok_in, cot, win, wout, wgate, wmix, gain1_in, gain2_in, cosine_in, signed_in,
-    lo_ref, tg_ref, ga_ref, gm_ref, gains_ref, *scratch
+    lo_ref, tg_ref, ga_ref, go_ref, gm_ref, gains_ref, *scratch
 ):
     names = list(SCRATCH) + ["s_" + n for n in SEMS]
     s = dict(zip(names, scratch, strict=True))
@@ -929,10 +851,12 @@
         load.start()
     loads[0].wait()
     loads[1].wait()
-    xhat, _ = norm(tok[...].astype(F32))
-    h1here = (xhat * gain1[...]).astype(BF)
-    r.h1here[...] = h1here
-    pl.when(jnp.logical_not(p.mover))(lambda: r.h1.__setitem__((own, slice(None)), h1here))
+    @pl.when(jnp.logical_not(p.mover))
+    def _():
+        xhat, _ = norm(tok[...].astype(F32))
+        r.h1[own, :] = (xhat * gain1[...]).astype(BF)
+        r.xb[...] = tok[...]
+
     r.qt[...] = jnp.zeros_like(r.qt)
     r.vt[:, 64:80, :] = jnp.ones((2, 16, T), BF)
     r.mt[FF:FR, :] = jnp.zeros((FR - FF, T), BF)
@@ -944,42 +868,46 @@
     sw_cot.start_near()
     pl.semaphore_wait(barrier, 24)
 
-    def sw_h(i):
-        return remote(
-            r.h1here.at[rows(i * 64, 64)],
-            r.h1.at[rows((2 * p.y + 1 - p.c) * B + i * 64, 64)],
-            r.s_sw_h.at[i],
-            r.s_sw_h.at[2 + i],
-            p.partner(),
-        )
+    def sw_x(i):
+        half = rows(i * 64, 64)
+        sems = r.s_sw_x
+        return remote(tok.at[half], r.xb.at[half], sems.at[i], sems.at[2 + i], p.partner())
+
+    def norm_half(i):
+        sw_x(i).wait()
+        xhat, _ = norm(r.xb[i * 64 : i * 64 + 64, :].astype(F32))
+        r.h1[rows(p.me * B + i * 64, 64), :] = (xhat * gain1[...]).astype(BF)
 
     f_w = Fetch(p, win, r.w, lambda role: rows(role * 128, 128 + role * 128), r.s_f_w)
-    f_wg = Fetch(p, wgate, r.wg, lambda i: (slice(None), slice(None), cols(i * 512, 512)), r.s_f_wg)
-    f_wm = Fetch(p, wmix, r.wm, lambda i: (slice(None), cols(i * 512, 512)), r.s_f_wm)
-    sw_x = Swap(p, tok, r.xb, r.s_sw_x)
+    f_wg = [
+        Fetch(p, wgate.at[i], r.wg.at[i], lambda role: (slice(None), pl.ds(512 * role, 512)), r.s_f_wg.at[i])
+        for i in range(2)
+    ]
+    f_wm = Fetch(p, wmix, r.wm, lambda role: (slice(None), pl.ds(256 * role, 256 + 512 * role)), r.s_f_wm)
     ag_h1, ag_h2, ag_gb = gather(r.h1, "h1"), gather(r.h2, "h2"), gather(r.gb, "gb")
     ag_cot = gather(r.cotb, "cot")
 
     @pl.when(p.mover)
     def _():
-        sw_h(0).start()
-        sw_h(1).start()
+        sw_x(0).start()
+        sw_x(1).start()
 
     f_w.start()
     pl.when(jnp.logical_not(p.mover))(lambda: ag_h1.start())
     whole_wo.w0()
     sw_cot.start_far()
+    f_wg[0].start()
+    f_wg[1].start()
 
     @pl.when(p.mover)
     def _():
-        sw_h(0).wait()
+        norm_half(0)
         ag_h1.start_top()
-        sw_h(1).wait()
+        norm_half(1)
         ag_h1.start_bottom()
 
     ag_h1.second()
     whole_wo.w1()
-    sw_x.start()
     f_w.wait()
     for load in loads[2:]:
         load.wait()
@@ -1006,12 +934,14 @@
         r.vt[1, 0:64, lanes] = vt[64:128]
 
     def early(step):
-        @pl.when(step == 3)
+        @pl.when(step == 1)
         def _():
             sw_cot.wait()
             ag_cot.start()
+
+        @pl.when(step == 3)
+        def _():
             whole_wo.w2()
-            f_wg.start()
             f_wm.start()
 
     ag_h1.steps(project, early, True)
@@ -1043,7 +973,6 @@
     r.orow[:, own_cols] = r.o[own, :]
     ag_cot.first()
     ag_cot.second()
-    sw_x.wait()
     whole_wo.w4()
     x_o.wait()
 
@@ -1057,7 +986,8 @@
     ag_h2.start()
     x_o.sent()
     ag_cot.third()
-    f_wg.wait()
+    f_wg[0].wait()
+    f_wg[1].wait()
     f_wm.wait()
     ag_cot.rest()
 
@@ -1089,8 +1019,8 @@
 
     rs_2 = scatter("r2")
     rs_2.phase(back_mix)
-    sums_m = PlaneSum(
-        p, r.gm, r.gm_big, r.gm_res, r.gm_small, r.gm_mine, r.gm_out, r.s_sm, r.s_sm_back, r.r2_part
+    sums_m = StagedPlaneSum(
+        p, r.gm, r.gm_big, r.gm_res, r.gm_small, r.gm_mine, r.gm_out, r.s_sm, r.s_sm_back
     )
 
     def mix_grads(i):
@@ -1104,22 +1034,18 @@
         r.gm[:, :, :, lanes] = jnp.concatenate(grads, 0).reshape(4, 4, 64, 256)
 
     pl.loop(0, 2)(mix_grads)
-    sums_m.first[0].s0()
+    sums_m.first[0].start()
     rs_2.step1()
     pl.loop(2, 4)(mix_grads)
-    sums_m.first[1].s0()
+    sums_m.first[1].start()
     dh2 = rs_2.step2()
-    sums_m.first[0].s1()
-    sums_m.first[1].s1()
 
     dx, dgain2 = norm_back(dh2, r.xhat2[...], r.inv2[...], gain2[...])
     gy = r.cotb[own, :].astype(F32) + dx
     r.gy[...] = gy
     r.gb[own, :] = gy.astype(BF)
     r.dorow[...] = nt(r.gb[own, :], r.wo[...]).astype(BF)
-    x_do = Exchange(
-        p, lambda j: r.dorow.at[:, cols(j * B, B)], r.dob.at[own], r.dob, r.s_x_do
-    )
+    x_do = Exchange(p, lambda j: r.dorow.at[:, cols(j * B, B)], r.dob.at[own], r.dob, r.s_x_do)
     x_do.start()
     r.dob[own, :] = r.dorow[:, own_cols]
     ag_gb.start()
@@ -1133,15 +1059,8 @@
         yy = (p.y + pick(step, 0, 3, 1, 2)) % 4
         at = rows(yy * 256, 256)
         lanes = cols(yy * 256, 256)
-
-        pl.when(step == 1)(sums_m.to_second)
-
-        @pl.when(step == 3)
-        def _():
-            sums_m.second[0].s1()
-            sums_m.second[1].s1()
-
         x_do.wait_pair(yy)
+        pl.when(step == 1)(lambda: sums_m.to_second(0))
         dot = r.dob[at, :].astype(F32).T
         zero = jnp.zeros((64, 256), BF)
         scaled = []
@@ -1161,6 +1080,7 @@
             r.dqt[half, lanes] = nn(r.kt[half, :], ds)
 
     x_do.sent()
+    sums_m.to_second(1)
 
     def back_project(yy):
         at = rows(yy * 256, 256)
@@ -1175,99 +1095,128 @@
         r.dqkvt[0:128, lanes] = dq.T.astype(BF)
         r.dqkvt[128:256, lanes] = dk.T.astype(BF)
         r.dqkvt[256:384, lanes] = dv.T.astype(BF)
-        dqkv = jnp.concatenate([dq.astype(BF), dk.astype(BF), dv.astype(BF)], 1)
-        return nn(dqkv, r.w[...])
-
+        r.dqkv[at, :] = jnp.concatenate([dq.astype(BF), dk.astype(BF), dv.astype(BF)], 1)
+
+    pl.loop(0, 4)(back_project)
+    gain_2.middle()
+
+    def spread_out(full, i, off, grad):
+        size = grad.shape[0] // 8
+        full[:, pl.ds(2 * i, 2), :, off : off + 256] = grad.astype(BF).reshape(4, 2, size, 256)
+
+    sums_a = PlaneSum(
+        p, r.ga, r.ga_big, r.ga_res, r.ga_small, r.ga_mine, r.ga_out, r.s_sa, r.s_sa_back
+    )
+    for n in range(2):
+
+        @pl.loop(0, 2)
+        def _(i, off=256 * n):
+            spread_out(r.ga, i, off, nn(r.dqkvt[...], r.h1[:, cols(i * 512 + off, 256)]))
+
+        sums_a.first[n].start()
+
+    sums_m.to_mine()
+    sums_m.g0()
+    ag_gb.first()
+    ag_gb.second()
     rs_1 = scatter("r1")
 
-    def late(step):
-        @pl.when(step == 0)
-        def _():
-            ag_gb.first()
-            ag_gb.second()
-
-        @pl.when(step == 1)
-        def _():
-            sums_m.to_mine()
-            sums_m.g0()
-
-    rs_1.phase(back_project, True, late)
+    rs_1.phase(lambda yy: nn(r.dqkv[rows(yy * 256, 256), :], r.w[...]))
     rs_1.step1()
+    sums_a.to_second(0, 1)
     sums_m.g1()
-    sums_a = Sums(
-        p, r.ga, r.ga_slots, r.ga_mine, r.ga_out, r.s_sa
-    )
     ag_gb.third()
     ag_gb.rest()
-
-    @pl.loop(0, 4)
-    def _(i):
-        off = (i + 2) % 4
-        lanes = cols(((p.z + off) % 4) * 256, 256)
-        r.ga[0:384, lanes] = nn(r.dqkvt[...], r.h1[:, lanes]).astype(BF)
-        r.ga[384:512, lanes] = nn(r.ot[...].astype(BF), r.gb[:, lanes]).astype(BF)
-        sums_a.spread(off)
+    sums_o = PlaneSum(
+        p, r.go, r.go_big, r.go_res, r.go_small, r.go_mine, r.go_out, r.s_so, r.s_so_back
+    )
+    for n in range(2):
+
+        @pl.loop(0, 2)
+        def _(i, off=256 * n):
+            spread_out(r.go, i, off, nn(r.ot[...].astype(BF), r.gb[:, cols(i * 512 + off, 256)]))
+
+        sums_o.first[n].start()
 
     rs_o.step0()
-    rs_o.step_right()
-    rs_o.step_left()
     dh1 = rs_1.step2()
     xhat, inverse = norm(r.xb[...].astype(F32))
     dx, dgain1 = norm_back(dh1, xhat, inverse, gain1[...])
     gain_1 = Gain(p, r.g1t, r.g1p, r.s_g1)
     gain_1.start(dgain1)
+    rs_o.step_right()
+    rs_o.step_left()
     r.tg_here[...] = (r.gy[...] + dx).astype(BF)
     sw_tg = Swap(p, r.tg_here, r.tg_out, r.s_sw_tg)
     sw_tg.start()
+    sums_a.to_mine()
+    sums_a.give()
+    sums_o.to_second(0, 1)
     sums_m.g2()
+    gain_1.middle()
     rs_o.step1()
-    sums_a.add()
-    sums_a.give()
-    gain_2.middle()
-    gain_1.middle()
+    sums_o.to_mine()
+    sums_o.give()
+    sums_m.g3()
     r.lo_here[...] = (r.y1[...] + rs_o.step2()).astype(BF)
     sw_lo = Swap(p, r.lo_here, r.lo_out, r.s_sw_lo)
     sw_lo.start()
     sw_tg.wait()
     tg_copy = pltpu.make_async_copy(r.tg_out, tg_ref, r.s_outs.at[0])
     tg_copy.start()
-    sums_m.g3()
-    sums_a.take()
+    sums_a.take(ga_ref, r.s_outs.at[3])
+    sums_o.take(go_ref, r.s_outs.at[4])
     sums_m.finish()
     gm_copy = pltpu.make_async_copy(r.gm_out, gm_ref, r.s_outs.at[1])
     gm_copy.start()
-    gains_ref[1:2, :] = gain_2.end()
-    gains_ref[0:1, :] = gain_1.end()
     sw_lo.wait()
     lo_copy = pltpu.make_async_copy(r.lo_out, lo_ref, r.s_outs.at[2])
     lo_copy.start()
-    sums_a.finish()
-    ga_copy = pltpu.make_async_copy(r.ga_out, ga_ref, r.s_outs.at[3])
-    ga_copy.start()
-    for copy in [lo_copy, tg_copy, gm_copy, ga_copy]:
+    gains_ref[1:2, :] = gain_2.end()
+    gains_ref[0:1, :] = gain_1.end()
+    sums_a.taken()
+    sums_o.taken()
+    for copy in [lo_copy, tg_copy, gm_copy]:
         copy.wait()
+    drain(r.ga_out, r.s_outs.at[3])
+    drain(r.go_out, r.s_outs.at[4])
 
 
 def widen(
-    lo, tg, ga, gm, gains, lo_ref, tg_ref, gi_ref, go_ref, gg_ref, gm_ref, first_ref, second_ref,
-    lo_in, tg_in, ga_in, gm_in, tg_out, ga_out, gm_out, sems,
+    lo, tg, ga, go, gm, gains, lo_ref, tg_ref, gi_ref, go_ref, gg_ref, gm_ref, first_ref, second_ref,
+    lo_in, tg_in, ga_in, go_in, gm_in, tg_out, ga_out, go_out, gm_out, sems,
 ):
-    pieces = [(gm, gm_in, gm_out, i * FR, FF, target) for i, target in enumerate((gm_ref, gg_ref.at[0], gg_ref.at[1]))]
-    pieces += [(ga, ga_in, ga_out, 0, 384, gi_ref), (ga, ga_in, ga_out, 384, B, go_ref)]
-    pieces += [(tg, tg_in, tg_out, 0, B, tg_ref)]
+    def whole(held, wide, first, size):
+        wide[first : first + size, :] = held[first : first + size, :].astype(F32)
+
+    def chunks(held, wide, first, size):
+        size = size // 8
+        for z in range(4):
+            for x in range(4):
+                group, half = (z * 2 + x % 2) * size, x // 2 * 512
+                wide[group : group + size, half : half + 512] = held[z, x].astype(F32)
+
+    targets = gm_ref, gg_ref.at[0], gg_ref.at[1]
+    pieces = [(gm, gm_in, gm_out, i * FR, FF, target, whole) for i, target in enumerate(targets)]
+    pieces += [
+        (ga, ga_in, ga_out, 0, 384, gi_ref, chunks),
+        (go, go_in, go_out, 0, B, go_ref, chunks),
+        (tg, tg_in, tg_out, 0, B, tg_ref, whole),
+    ]
     loads, stores = [], []
-    for i, (src, held, _, first, size, _) in enumerate(pieces):
-        part = pl.ds(first, FR if size == FF else size)
-        loads.append(pltpu.make_async_copy(src.at[part], held.at[part], sems.at[i]))
+    for i, (src, held, _, first, size, _, _) in enumerate(pieces):
+        if size == FF:
+            src, held = src.at[pl.ds(first, FR)], held.at[pl.ds(first, FR)]
+        loads.append(pltpu.make_async_copy(src, held, sems.at[i]))
     loads.append(pltpu.make_async_copy(lo, lo_in, sems.at[6]))
     for load in loads:
         load.start()
     for i in range(8):
         first_ref[i : i + 1, :] = gains[0:1, i * B : i * B + B]
         second_ref[i : i + 1, :] = gains[1:2, i * B : i * B + B]
-    for i, (_, held, wide, first, size, target) in enumerate(pieces):
+    for i, (_, held, wide, first, size, target, convert) in enumerate(pieces):
         loads[i].wait()
-        wide[first : first + size, :] = held[first : first + size, :].astype(F32)
+        convert(held, wide, first, size)
         stores.append(pltpu.make_async_copy(wide.at[pl.ds(first, size)], target, sems.at[7 + i]))
         stores[-1].start()
     loads[6].wait()
@@ -1282,13 +1231,13 @@
     any_space = pl.BlockSpec(memory_space=pl.ANY)
     vmem = pl.BlockSpec(memory_space=pltpu.VMEM)
     limit = 63 * 1024 * 1024
-    shapes = [(B, D), (B, D), (512, D), (4, 4, 64, D)]
-    lo, tg, ga, gm, gains = pl.pallas_call(
+    shapes = [(B, D), (B, D), (4, 4, 48, 512), (4, 4, 16, 512), (4, 4, 64, D)]
+    lo, tg, ga, go, gm, gains = pl.pallas_call(
         kernel,
         out_shape=tuple(jax.ShapeDtypeStruct(shape, BF) for shape in shapes)
         + (jax.ShapeDtypeStruct((2, D), F32),),
         in_specs=[any_space] * 10,
-        out_specs=(any_space,) * 4 + (vmem,),
+        out_specs=(any_space,) * 5 + (vmem,),
         scratch_shapes=[pltpu.VMEM(shape, kind) for shape, kind in SCRATCH.values()]
         + [pltpu.SemaphoreType.DMA(shape) for shape in SEMS.values()],
         compiler_params=pltpu.CompilerParams(
@@ -1311,20 +1260,22 @@
         widen,
         out_shape=(jax.ShapeDtypeStruct((B, D), BF),)
         + tuple(jax.ShapeDtypeStruct(shape, F32) for shape in wide),
-        in_specs=[any_space] * 4 + [vmem],
+        in_specs=[any_space] * 5 + [vmem],
         out_specs=(any_space,) * 6 + (vmem, vmem),
         scratch_shapes=[
             pltpu.VMEM((B, D), BF),
             pltpu.VMEM((B, D), BF),
-            pltpu.VMEM((512, D), BF),
+            pltpu.VMEM((4, 4, 48, 512), BF),
+            pltpu.VMEM((4, 4, 16, 512), BF),
             pltpu.VMEM((1024, D), BF),
             pltpu.VMEM((B, D), F32),
-            pltpu.VMEM((512, D), F32),
+            pltpu.VMEM((384, D), F32),
+            pltpu.VMEM((B, D), F32),
             pltpu.VMEM((3 * FR, D), F32),
             pltpu.SemaphoreType.DMA((14,)),
         ],
         compiler_params=pltpu.CompilerParams(vmem_limit_bytes=limit),
-    )(lo, tg, ga, gm.reshape(1024, D), gains)
+    )(lo, tg, ga, go, gm.reshape(1024, D), gains)
     return (
         lo,
         tg,

time: 126 us -> 120 us (0.952)
  Pallas kernels: 125 us -> 119 us
    pallas_call x1, Pallas kernels: 120 us -> 114 us  [local(): pl.pallas_call(kernel, out_shape=tuple((jax.ShapeDtypeStruct(shape, BF) f...]
where the time goes in v3:
time: 120 us
  Pallas kernels  119 us (99%)
    pallas_call x1, Pallas kernels, local(): pl.pallas_call(kernel, out_shape=tuple((jax.ShapeDtypeStruct(shape, BF) f...  114 us
    pallas_call x1, Pallas kernels, local(): pl.pallas_call(widen, out_shape=(jax.ShapeDtypeStruct((B, D), BF),) + tup...  5.47 us

profile of v3, /device:TPU:1, one launch (start us, length us, event | category | flops | bytes accessed | tf_op | source)
XLA Modules:
  0.0 119.8 jit_solution(867315123134819141)
XLA Ops:
  0.6 113.7 %shard_map.161 = (bf16[128,1024]{1,0:T(8,128)(2,1)}, bf16[128,1024]{1,0:T(8,128)(2,1)}, bf16[4,4,48,512]{3,2,1,0:T(8,128)(2,1)}, bf16[4,4,16,512]{3,2,1,0:T(8,12...) custom-call(bf16[128,1024]{1,0:T(8,128)(2,1)} %tok_in.1, bf16[128,1024]{1,0:T(8,128)(2,1)} %cot.1, ...), custom_call_target="tpu_custom_call" | custom-call | tf_op jit(solution)/shard_map/pallas_call | solution.py:1235
  114.3 5.5 %shard_map.162 = (bf16[128,1024]{1,0:T(8,128)(2,1)}, f32[128,1024]{1,0:T(8,128)}, f32[384,1024]{1,0:T(8,128)}, f32[128,1024]{1,0:T(8,128)}, f32[2,328,1024]{2,1,...) custom-call(bf16[128,1024]{1,0:T(8,128)(2,1)} %get-tuple-element.22.lo, ...), custom_call_target="tpu_custom_call" | custom-call | tf_op jit(solution)/shard_map/pallas_call | solution.py:1259

commit v4 on v3

--- a/solution.py
+++ b/solution.py
@@ -1098,7 +1098,6 @@
         r.dqkv[at, :] = jnp.concatenate([dq.astype(BF), dk.astype(BF), dv.astype(BF)], 1)
 
     pl.loop(0, 4)(back_project)
-    gain_2.middle()
 
     def spread_out(full, i, off, grad):
         size = grad.shape[0] // 8
@@ -1115,6 +1114,7 @@
 
         sums_a.first[n].start()
 
+    gain_2.middle()
     sums_m.to_mine()
     sums_m.g0()
     ag_gb.first()
@@ -1139,22 +1139,22 @@
         sums_o.first[n].start()
 
     rs_o.step0()
+    rs_o.step_right()
+    rs_o.step_left()
     dh1 = rs_1.step2()
     xhat, inverse = norm(r.xb[...].astype(F32))
     dx, dgain1 = norm_back(dh1, xhat, inverse, gain1[...])
     gain_1 = Gain(p, r.g1t, r.g1p, r.s_g1)
     gain_1.start(dgain1)
-    rs_o.step_right()
-    rs_o.step_left()
     r.tg_here[...] = (r.gy[...] + dx).astype(BF)
     sw_tg = Swap(p, r.tg_here, r.tg_out, r.s_sw_tg)
     sw_tg.start()
     sums_a.to_mine()
     sums_a.give()
     sums_o.to_second(0, 1)
+    rs_o.step1()
+    gain_1.middle()
     sums_m.g2()
-    gain_1.middle()
-    rs_o.step1()
     sums_o.to_mine()
     sums_o.give()
     sums_m.g3()
@@ -1164,11 +1164,11 @@
     sw_tg.wait()
     tg_copy = pltpu.make_async_copy(r.tg_out, tg_ref, r.s_outs.at[0])
     tg_copy.start()
-    sums_a.take(ga_ref, r.s_outs.at[3])
-    sums_o.take(go_ref, r.s_outs.at[4])
     sums_m.finish()
     gm_copy = pltpu.make_async_copy(r.gm_out, gm_ref, r.s_outs.at[1])
     gm_copy.start()
+    sums_a.take(ga_ref, r.s_outs.at[3])
+    sums_o.take(go_ref, r.s_outs.at[4])
     sw_lo.wait()
     lo_copy = pltpu.make_async_copy(r.lo_out, lo_ref, r.s_outs.at[2])
     lo_copy.start()
@@ -1196,13 +1196,13 @@
                 group, half = (z * 2 + x % 2) * size, x // 2 * 512
                 wide[group : group + size, half : half + 512] = held[z, x].astype(F32)
 
-    targets = gm_ref, gg_ref.at[0], gg_ref.at[1]
-    pieces = [(gm, gm_in, gm_out, i * FR, FF, target, whole) for i, target in enumerate(targets)]
-    pieces += [
-        (ga, ga_in, ga_out, 0, 384, gi_ref, chunks),
+    pieces = [
         (go, go_in, go_out, 0, B, go_ref, chunks),
         (tg, tg_in, tg_out, 0, B, tg_ref, whole),
+        (ga, ga_in, ga_out, 0, 384, gi_ref, chunks),
     ]
+    targets = gm_ref, gg_ref.at[0], gg_ref.at[1]
+    pieces += [(gm, gm_in, gm_out, i * FR, FF, target, whole) for i, target in enumerate(targets)]
     loads, stores = [], []
     for i, (src, held, _, first, size, _, _) in enumerate(pieces):
         if size == FF:

time: 120 us -> 121 us (level)
  no operation moved by 1% of the time
where the time goes in v4:
time: 121 us
  Pallas kernels  120 us (99%)
    pallas_call x1, Pallas kernels, local(): pl.pallas_call(kernel, out_shape=tuple((jax.ShapeDtypeStruct(shape, BF) f...  115 us
    pallas_call x1, Pallas kernels, local(): pl.pallas_call(widen, out_shape=(jax.ShapeDtypeStruct((B, D), BF),) + tup...  5.33 us

profile of v4, /device:TPU:1, one launch (start us, length us, event | category | flops | bytes accessed | tf_op | source)
XLA Modules:
  0.0 120.5 jit_solution(10160842130752452571)
XLA Ops:
  0.6 114.6 %shard_map.161 = (bf16[128,1024]{1,0:T(8,128)(2,1)}, bf16[128,1024]{1,0:T(8,128)(2,1)}, bf16[4,4,48,512]{3,2,1,0:T(8,128)(2,1)}, bf16[4,4,16,512]{3,2,1,0:T(8,12...) custom-call(bf16[128,1024]{1,0:T(8,128)(2,1)} %tok_in.1, bf16[128,1024]{1,0:T(8,128)(2,1)} %cot.1, ...), custom_call_target="tpu_custom_call" | custom-call | tf_op jit(solution)/shard_map/pallas_call | solution.py:1235
  115.2 5.3 %shard_map.162 = (bf16[128,1024]{1,0:T(8,128)(2,1)}, f32[128,1024]{1,0:T(8,128)}, f32[384,1024]{1,0:T(8,128)}, f32[128,1024]{1,0:T(8,128)}, f32[2,328,1024]{2,1,...) custom-call(bf16[128,1024]{1,0:T(8,128)(2,1)} %get-tuple-element.22.lo, ...), custom_call_target="tpu_custom_call" | custom-call | tf_op jit(solution)/shard_map/pallas_call | solution.py:1259
